TPU v7x, 32 devices: a whole 2x2x4 slice. The times are simulated.
32 devices in a mesh: freq: 4 (over z), row: 8 (over y, x, core).
Axes of the slice: x: 2, y: 2, z: 4, core: 2. Of those that a mesh axis runs over, the one named last changes fastest.
Arguments:
- vis_values: bfloat16 [4, 512, 2, 128], P('freq', 'row'), may hold values from -6 to 6
- kernel_u: bfloat16 [4, 512, 7, 128], P('freq', 'row'), may hold values from 0.049804688 to 1
- kernel_v: bfloat16 [4, 512, 7, 128], P('freq', 'row'), may hold values from 0.049804688 to 1
- offset_u: int32 [4, 512, 128], P('freq', 'row'), may hold values from 0 to 9
- offset_v: int32 [4, 512, 128], P('freq', 'row'), may hold values from 0 to 121
- block_owner: int32 [4, 512, 1], P('freq', 'row'), may hold values from 0 to 7; in each aligned block of 64 rows (0 to 63, 64 to 127, ..., all dimensions but the last counted through in order) at most 32 rows name the same one
- tile_slot: int32 [4, 512], P('freq', 'row'), may hold values from 0 to 1023
- channel_freq: float32 [4], P('freq'), may hold values from 0.856 to 1.712
Outputs:
- taylor: bfloat16 [3, 4096, 4096], P(None, 'freq', 'row')
Inputs may be any that keep to these rules, and one draw needn't show every extreme that they name: `block_owner`: among the 64 blocks of one channel held by one index of row, at most 32 name the same owner, a bound that some block reaches.
All inputs are finite; a program needn't handle non-finite values.
Results may differ from a plain program's by a relative error of at most 0.024.
Values may be sent and summed in bfloat16 or wider, within the bound.
A program may use at most 128 MiB of HBM per device.

v0:
```python
from functools import partial
import math

import jax
import jax.numpy as jnp
from jax import lax
from jax.sharding import PartitionSpec as P

GRID = 4096
TU = 16
TV = 128


def for_sending(shard):
    return jax.tree.map(lambda a: a.astype(jnp.bfloat16) if a.dtype == jnp.float32 else a, shard)


def dft_tables(length):
    outer_len = 32
    inner_len = length // outer_len
    index_outer = jnp.arange(outer_len, dtype=jnp.int32)
    index_inner = jnp.arange(inner_len, dtype=jnp.int32)
    full_turn = 2.0 * math.pi
    angle_outer = (
        full_turn
        * (index_outer[:, None] * index_outer[None, :] % outer_len).astype(jnp.float32)
        / outer_len
    )
    angle_twist = (
        full_turn
        * (index_outer[:, None] * index_inner[None, :] % length).astype(jnp.float32)
        / length
    )
    angle_inner = (
        full_turn
        * (index_inner[:, None] * index_inner[None, :] % inner_len).astype(jnp.float32)
        / inner_len
    )
    return (
        jnp.cos(angle_outer),
        jnp.sin(angle_outer),
        jnp.cos(angle_twist),
        jnp.sin(angle_twist),
        jnp.cos(angle_inner),
        jnp.sin(angle_inner),
    )


def transform_last(real_part, imag_part):
    row_total, length = real_part.shape
    outer_len = 32
    inner_len = length // outer_len
    cos_outer, sin_outer, cos_twist, sin_twist, cos_inner, sin_inner = dft_tables(length)
    product = partial(jnp.einsum, precision=lax.Precision.HIGHEST)
    real_part = real_part.reshape(row_total, outer_len, inner_len)
    imag_part = imag_part.reshape(row_total, outer_len, inner_len)
    step_real = product("rab,ak->rkb", real_part, cos_outer) - product(
        "rab,ak->rkb", imag_part, sin_outer
    )
    step_imag = product("rab,ak->rkb", real_part, sin_outer) + product(
        "rab,ak->rkb", imag_part, cos_outer
    )
    twist_real = step_real * cos_twist - step_imag * sin_twist
    twist_imag = step_real * sin_twist + step_imag * cos_twist
    out_real = product("rkb,bm->rmk", twist_real, cos_inner) - product(
        "rkb,bm->rmk", twist_imag, sin_inner
    )
    out_imag = product("rkb,bm->rmk", twist_real, sin_inner) + product(
        "rkb,bm->rmk", twist_imag, cos_inner
    )
    return (out_real.reshape(row_total, length), out_imag.reshape(row_total, length))


def transform_first_real(real_part, imag_part):
    length, col_total = real_part.shape
    outer_len = 32
    inner_len = length // outer_len
    cos_outer, sin_outer, cos_twist, sin_twist, cos_inner, sin_inner = dft_tables(length)
    product = partial(jnp.einsum, precision=lax.Precision.HIGHEST)
    real_part = real_part.reshape(outer_len, inner_len, col_total)
    imag_part = imag_part.reshape(outer_len, inner_len, col_total)
    step_real = product("abc,ak->kbc", real_part, cos_outer) - product(
        "abc,ak->kbc", imag_part, sin_outer
    )
    step_imag = product("abc,ak->kbc", real_part, sin_outer) + product(
        "abc,ak->kbc", imag_part, cos_outer
    )
    twist_real = step_real * cos_twist[:, :, None] - step_imag * sin_twist[:, :, None]
    twist_imag = step_real * sin_twist[:, :, None] + step_imag * cos_twist[:, :, None]
    out_real = product("kbc,bm->mkc", twist_real, cos_inner) - product(
        "kbc,bm->mkc", twist_imag, sin_inner
    )
    return out_real.reshape(length, col_total)


def grid_blocks(payload, offsets):
    tap_count = (payload.shape[1] - 2) // 2
    values = payload[:, :2, :].astype(jnp.float32)
    kern_u = payload[:, 2 : 2 + tap_count, :]
    kern_v = payload[:, 2 + tap_count :, :]
    row_grid = jnp.arange(TU, dtype=jnp.int32)[None, :, None]
    col_grid = jnp.arange(TV, dtype=jnp.int32)[None, None, :]
    spread_u = jnp.zeros((payload.shape[0], TU, payload.shape[2]), jnp.float32)
    spread_v = jnp.zeros((payload.shape[0], payload.shape[2], TV), jnp.bfloat16)
    for tap_index in range(tap_count):
        spread_u = spread_u + jnp.where(
            row_grid == offsets[:, 0:1, :] + tap_index,
            kern_u[:, tap_index : tap_index + 1, :].astype(jnp.float32),
            0.0,
        )
        spread_v = jnp.where(
            col_grid == offsets[:, 1, :, None] + tap_index, kern_v[:, tap_index, :, None], spread_v
        )
    left = (values[:, :, None, :] * spread_u[:, None, :, :]).astype(jnp.bfloat16)
    return jnp.einsum("spin,snj->spij", left, spread_v, preferred_element_type=jnp.float32)


def shards(
    vis_values, kernel_u, kernel_v, offset_u, offset_v, block_owner, tile_slot, channel_freq
):
    row_count = lax.axis_size("row")
    block_count = vis_values.shape[1]
    vis_count = vis_values.shape[3]
    capacity = max(2, 4 * block_count // row_count)
    slot_count = row_count * capacity
    slab_rows = GRID // row_count
    tiles_total = slab_rows // TU * (GRID // TV)
    owner_row = block_owner[0, :, 0]
    row_marks = (owner_row[:, None] == jnp.arange(row_count, dtype=jnp.int32)[None, :]).astype(
        jnp.int32
    )
    before = jnp.cumsum(row_marks, axis=0) - row_marks
    slot_rank = jnp.sum(before * row_marks, axis=1)
    target = owner_row * capacity + slot_rank
    payload = jnp.concatenate([vis_values[0], kernel_u[0], kernel_v[0]], axis=1)
    offsets = jnp.stack([offset_u[0], offset_v[0]], axis=1)
    send_tile = jnp.full((slot_count,), tiles_total, jnp.int32).at[target].set(tile_slot[0])
    send_tile = send_tile.reshape(row_count, capacity)
    send_payload = (
        jnp.zeros((slot_count,) + payload.shape[1:], jnp.bfloat16).at[target].set(payload)
    )
    send_offsets = jnp.zeros((slot_count,) + offsets.shape[1:], jnp.int32).at[target].set(offsets)
    recv_payload, recv_offsets, recv_tile = (
        lax.all_to_all(
            send_payload.reshape((row_count, capacity) + payload.shape[1:]),
            "row",
            split_axis=0,
            concat_axis=0,
            tiled=True,
        ),
        lax.all_to_all(
            send_offsets.reshape((row_count, capacity) + offsets.shape[1:]),
            "row",
            split_axis=0,
            concat_axis=0,
            tiled=True,
        ),
        lax.all_to_all(send_tile, "row", split_axis=0, concat_axis=0, tiled=True),
    )
    contribution = grid_blocks(
        recv_payload.reshape((slot_count,) + payload.shape[1:]),
        recv_offsets.reshape((slot_count,) + offsets.shape[1:]),
    )
    slab_tiles = (
        jnp.zeros((tiles_total, 2, TU, TV), jnp.float32)
        .at[recv_tile.reshape(-1)]
        .add(contribution, mode="drop")
    )
    slab_grid = (
        slab_tiles.reshape(slab_rows // TU, GRID // TV, 2, TU, TV)
        .transpose(2, 0, 3, 1, 4)
        .reshape(2, slab_rows, GRID)
    )
    spec_real, spec_imag = transform_last(slab_grid[0], slab_grid[1])
    spectrum = jnp.stack([spec_real, spec_imag]).reshape(2, slab_rows, row_count, GRID // row_count)
    image_scale = 1.0 / math.sqrt(block_count * row_count * vis_count)
    offset_freq = (channel_freq[0] - 1.284) / 0.428
    weights = jnp.stack([jnp.ones_like(offset_freq), offset_freq, offset_freq * offset_freq])
    received = lax.all_to_all(
        for_sending(spectrum), "row", split_axis=2, concat_axis=1, tiled=True
    ).astype(spectrum.dtype)
    width_here = received.shape[2] * received.shape[3]
    real_cols = received[0].reshape(GRID, width_here)
    imag_cols = received[1].reshape(GRID, width_here)
    dirty_image = transform_first_real(real_cols, imag_cols) * image_scale
    taylor_terms = (weights[:, None, None] * dirty_image[None]).astype(jnp.bfloat16)
    terms_all = taylor_terms.reshape(3, GRID, received.shape[2], received.shape[3])
    terms_all = terms_all.reshape(3, GRID, GRID // row_count).astype(jnp.float32)
    summed = lax.psum_scatter(
        terms_all.astype(jnp.bfloat16), "freq", scatter_dimension=1, tiled=True
    )
    return summed


def solution(mesh):
    return jax.shard_map(
        shards,
        mesh=mesh,
        in_specs=(
            P("freq", "row", None, None),
            P("freq", "row", None, None),
            P("freq", "row", None, None),
            P("freq", "row", None),
            P("freq", "row", None),
            P("freq", "row", None),
            P("freq", "row"),
            P("freq"),
        ),
        out_specs=P(None, "freq", "row"),
        check_vma=False,
    )
```

profile of v0, /device:TPU:16, one launch (start us, length us, event | category | flops | bytes accessed | tf_op | source)
XLA Modules:
  0.0 784.9 jit_solution(785265537580375577)
XLA Ops:
  6.5 0.7 fusion.74
  7.4 0.8 select_reduce_fusion
  8.2 0.7 fusion.119
  8.9 0.9 scatter_custom_fusion
  9.8 0.7 all_to_all.23
  10.5 3.7 all-to-all-start
  14.2 0.8 pad_add_fusion
  15.0 0.8 broadcast_in_dim.180
  15.8 6.5 scatter_fusion.1
  22.3 4.2 all-to-all-start.2
  26.5 0.8 copy.99
  27.2 1.0 pad_maximum_fusion.1
  28.4 1.1 broadcast_in_dim.179
  29.5 6.8 scatter_fusion
  36.3 4.2 all-to-all-start.1
  42.5 13.5 %all-to-all-done.1 = bf16[8,32,16,128]{3,2,1,0:T(8,128)(2,1)S(1)} async-done(((bf16[8,32,16,128]{3,2,1,0:T(8,128)(2,1)}), bf16[8,32,16,128]{3,2,1,0:T(8,128)(2,1)S(1)}, u32[]{:S(2)}, u32[]{:S(2)}) %all-to-all-start.1) | async-done | bytes 1048608 | tf_op jit(solution)/shard_map/all_to_all | solution.py:144
  56.6 1.8 select_add_fusion
  58.4 109.5 %fusion.8 = f32[256,2,16,128]{3,2,1,0:T(8,128)} fusion(s32[256,128]{1,0:T(8,128)S(1)} %bitcast.172, s32[256,128]{1,0:T(8,128)S(1)} %get-tuple-element.36, s32[256,128]{1,0:T(8,128)S(1)} %get-tuple-element.37, s32[256,128]{1,0:T(8,128)S(1)} %get-tuple-element.38, s32[256,128]{1,0:T(8,128)S(1)} %get-tuple-element.39, s32[256,128]{1,0:T(8,128)S(1)} %get-tuple-element.40, ...), kind=kOutput, calls=%fused_computation.20 | convolution fusion | flops 329252864 | bytes 7929856 | tf_op jit(solution)/shard_map/spin,snj->spij/dot_general | solution.py:115
  167.9 7.9 %broadcast_in_dim.178 = f32[1024,2,16,128]{3,2,1,0:T(8,128)} broadcast(f32[]{:T(128)} %constant.107.clone.1), dimensions={} | broadcast | bytes 16777220 | tf_op jit(solution)/shard_map/broadcast_in_dim | solution.py:165
  175.8 30.5 %scatter_fusion.2 = f32[1024,2,16,128]{3,2,1,0:T(8,128)} fusion(f32[1024,2,16,128]{3,2,1,0:T(8,128)} %broadcast_in_dim.178, s32[256]{0:T(256)S(1)} %bitcast.185, f32[256,2,16,128]{3,2,1,0:T(8,128)} %fusion.8), kind=kCustom, calls=%fused_computation.3 | custom fusion | flops 1048576 | bytes 12583936 | tf_op jit(solution)/shard_map/scatter-add | solution.py:167
  206.3 10.1 %fusion.179 = (f32[1,32,16,32,128]{4,2,0,3,1:T(8,128)}, f32[1,32,16,32,128]{4,2,0,3,1:T(8,128)S(1)}) fusion(f32[2,32,16,32,128]{4,2,0,3,1:T(8,128)} %bitcast.153), kind=kLoop, calls=%fused_computation.232 | loop fusion | bytes 33554432 | tf_op jit(solution)/shard_map/slice | solution.py:174
  216.4 6.8 copy.50
  223.2 9.7 %fusion.97 = f32[32,512,128]{2,0,1:T(8,128)} fusion(f32[512,32,128]{2,1,0:T(8,128)S(1)} %bitcast.154), kind=kOutput, calls=%fused_computation.154 | convolution fusion | flops 805320704 | bytes 16777216 | tf_op jit(solution)/shard_map/rab,ak->rkb/dot_general | solution.py:60
  233.0 9.5 %fusion.93 = f32[32,512,128]{2,0,1:T(8,128)} fusion(f32[512,32,128]{2,1,0:T(8,128)S(1)} %bitcast.155), kind=kOutput, calls=%fused_computation.150 | convolution fusion | flops 805320704 | bytes 16777216 | tf_op jit(solution)/shard_map/rab,ak->rkb/dot_general | solution.py:57
  242.5 3.5 copy.49
  245.9 9.7 %fusion.91 = f32[32,512,128]{2,0,1:T(8,128)} fusion(f32[512,32,128]{2,1,0:T(8,128)S(1)} %bitcast.158), kind=kOutput, calls=%fused_computation.148 | convolution fusion | flops 805320704 | bytes 16777216 | tf_op jit(solution)/shard_map/rab,ak->rkb/dot_general | solution.py:60
  255.6 19.1 %subtract_bitcast_fusion = (f32[512,32,128]{2,1,0:T(8,128)}, f32[512,32,128]{2,1,0:T(8,128)}) fusion(f32[32,128]{1,0:T(8,128)S(1)} %get-tuple-element.41, f32[32,128]{1,0:T(8,128)S(1)} %get-tuple-element.42, f32[32,512,128]{2,0,1:T(8,128)} %fusion.91, f32[32,512,128]{2,0,1:T(8,128)} %fusion.97, f32[32,512,128]{2,0,1:T(8,128)} %fusion.93, ...), kind=kOutput, calls=%fused_computation.32 | convolution fusion | flops 822097920 | bytes 50364416 | tf_op jit(solution)/shard_map/rab,ak->rkb/dot_general | solution.py:57
  274.7 21.6 %fusion.21 = f32[128,512,32]{1,0,2:T(8,128)} fusion(f32[512,32,128]{2,1,0:T(8,128)} %get-tuple-element.8), kind=kOutput, calls=%fused_computation.40 | convolution fusion | flops 3221454848 | bytes 16777216 | tf_op jit(solution)/shard_map/rkb,bm->rmk/dot_general | solution.py:68
  296.4 15.6 %fusion.23 = f32[128,512,32]{1,0,2:T(8,128)S(1)} fusion(f32[512,32,128]{2,1,0:T(8,128)S(1)} %copy-done.1), kind=kOutput, calls=%fused_computation.42 | convolution fusion | flops 3221454848 | bytes 16777216 | tf_op jit(solution)/shard_map/rkb,bm->rmk/dot_general | solution.py:65
  312.0 15.9 %fusion.30 = bf16[512,128,32]{0,1,2:T(8,128)(2,1)} fusion(f32[128,512,32]{1,0,2:T(8,128)} %fusion.21, f32[512,32,128]{2,1,0:T(8,128)S(1)} %bitcast.157), kind=kOutput, calls=%fused_computation.49 | convolution fusion | flops 3225649152 | bytes 20971520 | tf_op jit(solution)/shard_map/rkb,bm->rmk/dot_general | solution.py:68
  327.9 6.5 copy.56
  334.4 13.7 %fusion.29 = bf16[512,128,32]{0,1,2:T(8,128)(2,1)} fusion(f32[128,512,32]{1,0,2:T(8,128)S(1)} %fusion.23, f32[512,32,128]{2,1,0:T(8,128)S(1)} %bitcast.157), kind=kOutput, calls=%fused_computation.48 | convolution fusion | flops 3225649152 | bytes 20971520 | tf_op jit(solution)/shard_map/rkb,bm->rmk/dot_general | solution.py:65
  348.1 6.6 copy.53
  354.7 6.2 pad_maximum_fusion
  360.9 7.3 copy.57
  368.3 4.9 all-to-all-start.3
  374.2 93.1 %all-to-all-done.3 = bf16[2,512,8,512]{1,3,0,2:T(8,128)(2,1)} async-done(((bf16[2,512,8,512]{1,3,0,2:T(8,128)(2,1)}), bf16[2,512,8,512]{1,3,0,2:T(8,128)(2,1)}, u32[]{:S(2)}, u32[]{:S(2)}) %all-to-all-start.3) | async-done | bytes 8388640 | tf_op jit(solution)/shard_map/all_to_all | solution.py:179
  467.3 11.8 %copy.58 = bf16[2,512,8,512]{3,1,2,0:T(8,128)(2,1)} copy(bf16[2,512,8,512]{1,3,0,2:T(8,128)(2,1)} %all-to-all-done.3) | data formatting | bytes 16777216 | tf_op jit(solution)/shard_map/all_to_all | solution.py:179
  479.1 3.8 fusion.180
  483.0 6.9 fusion.39
  489.9 6.9 fusion.41
  496.8 7.0 fusion.45
  503.8 19.1 %multiply_subtract_fusion = (f32[32,128,512]{2,0,1:T(8,128)}, f32[32,128,512]{2,0,1:T(8,128)}) fusion(f32[32,128]{0,1:T(8,128)S(1)} %copy.64, f32[32,128]{0,1:T(8,128)S(1)} %copy.61, f32[32,128,512]{2,0,1:T(8,128)} %fusion.39, f32[32,128,512]{2,0,1:T(8,128)} %fusion.45, f32[32,128,512]{2,0,1:T(8,128)} %fusion.41, bf16[32,128,512]{2,1,0:T(8,128)(2,1)} %bitcast.163), kind=kOutput, calls=%fused_computation.28 | convolution fusion | flops 822097920 | bytes 46170112 | tf_op jit(solution)/shard_map/abc,ak->kbc/dot_general | solution.py:85
  522.9 17.2 %fusion.10 = f32[128,32,512]{2,0,1:T(8,128)S(1)} fusion(f32[32,128,512]{2,0,1:T(8,128)} %get-tuple-element.6), kind=kOutput, calls=%fused_computation.22 | convolution fusion | flops 3221454848 | bytes 16777216 | tf_op jit(solution)/shard_map/kbc,bm->mkc/dot_general | solution.py:90
  540.1 12.6 %subtract_multiply_fusion = f32[128,32,512]{2,0,1:T(8,128)S(1)} fusion(f32[128,32,512]{2,0,1:T(8,128)S(1)} %fusion.10, f32[32,128,512]{2,0,1:T(8,128)S(1)} %copy-done.3), kind=kOutput, calls=%fused_computation.26 | convolution fusion | flops 3225649152 | bytes 25165824 | tf_op jit(solution)/shard_map/kbc,bm->mkc/dot_general | solution.py:90
  552.8 4.9 copy.67
  557.6 7.3 multiply_convert_fusion
  565.0 212.8 %reduce-scatter.2.cloned.1.call-done = bf16[3,1024,512]{2,1,0:T(8,128)(2,1)} async-done(((bf16[3,4096,512]{2,1,0:T(8,128)(2,1)}), bf16[3,1024,512]{2,1,0:T(8,128)(2,1)}) %reduce-scatter.2.cloned.1.call-update) | async-done | bytes 3145744 | tf_op jit(solution)/shard_map/reduce_scatter | solution.py:189
  (36 shorter events, 3.2 us)
Async XLA Ops:
  10.5 11.8 %all-to-all-start = ((s32[8,1,32]{2,1,0:T(1,128)}), s32[8,1,32]{2,1,0:T(1,128)S(1)}, u32[]{:S(2)}, u32[]{:S(2)}) async-start(s32[8,1,32]{2,1,0:T(1,128)} %all_to_all.23), calls=%async_computation | async-start | bytes 8192 | tf_op jit(solution)/shard_map/all_to_all | solution.py:158
  22.3 14.1 %all-to-all-start.2 = ((s32[8,32,2,128]{3,2,1,0:T(2,128)}), s32[8,32,2,128]{3,2,1,0:T(2,128)S(1)}, u32[]{:S(2)}, u32[]{:S(2)}) async-start(s32[8,32,2,128]{3,2,1,0:T(2,128)} %bitcast.15), calls=%async_computation.2 | async-start | bytes 524288 | tf_op jit(solution)/shard_map/all_to_all | solution.py:151
  36.3 19.6 %all-to-all-start.1 = ((bf16[8,32,16,128]{3,2,1,0:T(8,128)(2,1)}), bf16[8,32,16,128]{3,2,1,0:T(8,128)(2,1)S(1)}, u32[]{:S(2)}, u32[]{:S(2)}) async-start(bf16[8,32,16,128]{3,2,1,0:T(8,128)(2,1)} %bitcast.11), calls=%async_computation.1 | async-start | bytes 2097152 | tf_op jit(solution)/shard_map/all_to_all | solution.py:144
  245.9 9.7 %copy-start = (f32[1,32,16,32,128]{4,3,2,1,0:T(8,128)}, f32[1,32,16,32,128]{4,3,2,1,0:T(8,128)S(1)}, u32[]{:S(2)}) copy-start(f32[1,32,16,32,128]{4,3,2,1,0:T(8,128)S(1)} %copy.49) | copy-start | bytes 25165828
  274.7 21.7 %copy-start.1 = (f32[512,32,128]{2,1,0:T(8,128)S(1)}, f32[512,32,128]{2,1,0:T(8,128)}, u32[]{:S(2)}) copy-start(f32[512,32,128]{2,1,0:T(8,128)} %get-tuple-element.8) | copy-start | bytes 25165828
  274.7 37.3 %slice-start = ((s8[8388608]{0:T(1024)(128)(4,1)}), s8[4194304]{0:T(1024)(128)(4,1)S(1)}, s32[]{:S(2)}) async-start(s8[8388608]{0:T(1024)(128)(4,1)} %bitcast.156), calls=%async_computation.6 | async-start | bytes 8388608
  296.4 15.6 %slice-start.1 = ((s8[8388608]{0:T(1024)(128)(4,1)}), s8[4194304]{0:T(1024)(128)(4,1)S(1)}, s32[]{:S(2)}) async-start(s8[8388608]{0:T(1024)(128)(4,1)} %bitcast.156), calls=%async_computation.7 | async-start | bytes 8388608
  348.1 6.7 copy-start.4
  368.3 99.0 %all-to-all-start.3 = ((bf16[2,512,8,512]{1,3,0,2:T(8,128)(2,1)}), bf16[2,512,8,512]{1,3,0,2:T(8,128)(2,1)}, u32[]{:S(2)}, u32[]{:S(2)}) async-start(bf16[2,512,8,512]{1,3,0,2:T(8,128)(2,1)} %copy.57), calls=%async_computation.3 | async-start | bytes 16777216 | tf_op jit(solution)/shard_map/all_to_all | solution.py:179
  373.2 404.6 %reduce-scatter.2.cloned.1.call-start = ((), (), s32[]{:S(2)}) async-start(), calls=%async_computation.5 | async-start | bytes 15728640 | tf_op jit(solution)/shard_map/reduce_scatter | solution.py:189
  483.0 13.8 %copy-start.2 = (bf16[1,8,512,1,512]{4,2,1,3,0:T(8,128)(2,1)}, bf16[1,8,512,1,512]{4,2,1,3,0:T(8,128)(2,1)S(1)}, u32[]{:S(2)}) copy-start(bf16[1,8,512,1,512]{4,2,1,3,0:T(8,128)(2,1)S(1)} %get-tuple-element.12) | copy-start | bytes 12582916
  522.9 17.2 %copy-start.3 = (f32[32,128,512]{2,0,1:T(8,128)S(1)}, f32[32,128,512]{2,0,1:T(8,128)}, u32[]{:S(2)}) copy-start(f32[32,128,512]{2,0,1:T(8,128)} %get-tuple-element.5) | copy-start | bytes 25165828
Sparse Core Ops, SparseCore 0:
  565.1 212.6 reduce-scatter.1
where the time goes:
time: 795 us; the launch traced here: 785 us
  waiting for transfers between devices  319 us (40%)
  matrix products  294 us (37%)
  local copies, waits for them, and re-layouts  88.3 us (11%)
  other arithmetic  51.5 us (6%)
  starting transfers between devices  17.1 us (2%)
  between operations  14.5 us (2%)
    reduce_scatter x1, waiting for transfers between devices, shards(): lax.psum_scatter(terms_all.astype(jnp.bfloat16), 'freq', scatter_dimensio...  213 us
    dot_general x1, matrix products, grid_blocks(): jnp.einsum('spin,snj->spij', left, spread_v, preferred_element_type=jnp.f...  109 us
    all_to_all x1, waiting for transfers between devices, shards(): lax.all_to_all(for_sending(spectrum), 'row', split_axis=2, concat_axis=1,...  93.1 us
    scatter-add x1, other arithmetic, shards(): slab_tiles = jnp.zeros((tiles_total, 2, TU, TV), jnp.float32).at[recv_til...  30.5 us
    dot_general x1, matrix products, transform_last(): product('rkb,bm->rmk', twist_imag, cos_inner)  21.6 us
    slice x3, local copies, waits for them, and re-layouts, shards(): spec_real, spec_imag = transform_last(slab_grid[0], slab_grid[1])  20.4 us
    dot_general x1, matrix products, transform_first_real(): product('abc,ak->kbc', real_part, sin_outer)  19.1 us
    dot_general x1, matrix products, transform_last(): product('rab,ak->rkb', real_part, cos_outer)  19.1 us
  transfers between devices with their start and end apart: 5, of which 3 were waited for; matrix products, arithmetic and copies ran while one was open for 3% of the time, Pallas kernels for 0%

commit v1 on v0

v1 whole, which is shorter than its diff:
```python
import math

import jax
import jax.numpy as jnp
import ml_dtypes
import numpy as np
from jax import lax
from jax.experimental import pallas as pl
from jax.experimental.pallas import tpu as pltpu
from jax.sharding import PartitionSpec as P

GRID = 4096
TU = 16
TV = 128
BANDS = GRID // TU
TILE_COLS = GRID // TV
BF16 = ml_dtypes.bfloat16
VMEM_LIMIT = 56 * 1024 * 1024


def turn(index, length):
    angle = 2.0 * np.pi * (index % length) / length
    return np.cos(angle), np.sin(angle)


def tile_tables(row_count):
    width = GRID // row_count
    j = np.arange(TV)[:, None]
    m = np.arange(GRID)[None, :]
    cos, sin = turn(j * m, GRID)
    cos = cos.reshape(TV, row_count, width).transpose(1, 0, 2)
    sin = sin.reshape(TV, row_count, width).transpose(1, 0, 2)
    top = np.concatenate([cos, sin], axis=2)
    low = np.concatenate([-sin, cos], axis=2)
    return np.concatenate([top, low], axis=1).astype(BF16)


def phase_table(width):
    cos, sin = turn(np.arange(TILE_COLS)[:, None] * np.arange(width)[None, :], TILE_COLS)
    return np.stack([cos, sin], axis=1).reshape(2 * TILE_COLS, width).astype(np.float32)


def band_table(scale):
    index = np.arange(BANDS)
    cos, sin = turn(index[:, None] * index[None, :], BANDS)
    return (np.block([[cos, -sin], [sin, cos]]) * scale).astype(BF16)


def inner_table():
    groups = BANDS // 16
    g = np.arange(groups)[:, None, None, None]
    high = np.arange(TU)[None, :, None, None]
    low = np.arange(16)[None, None, :, None]
    i = np.arange(TU)[None, None, None, :]
    cos, sin = turn(i * (16 * g + low + BANDS * high), GRID)
    parts = np.stack([cos, -sin], axis=4)
    full = parts[..., None] * np.eye(16)[None, None, :, None, None, :]
    return full.reshape(groups, TU * 16, TU * 2 * 16).astype(BF16)


def grid_kernel(vis_ref, ku_ref, kv_ref, ou_ref, ov_ref, ids_ref, out_ref):
    blocks, taps = ku_ref.shape[0], ku_ref.shape[1]

    def one(b, carry):
        d_u = lax.broadcasted_iota(jnp.int32, (TU, TV), 0) - ou_ref[pl.ds(b, 1), :]
        d_v = lax.broadcasted_iota(jnp.int32, (TV, TV), 0) - ov_ref[pl.ds(b, 1), :]
        ku = ku_ref[b].astype(jnp.float32)
        kv = kv_ref[b].astype(jnp.float32)
        vis = vis_ref[b].astype(jnp.float32)
        spread_u = jnp.zeros((TU, TV), jnp.float32)
        spread_v = jnp.zeros((TV, TV), jnp.float32)
        for t in range(taps):
            spread_u = jnp.where(d_u == t, ku[t : t + 1], spread_u)
            spread_v = jnp.where(d_v == t, kv[t : t + 1], spread_v)
        left = jnp.concatenate([vis[0:1] * spread_u, vis[1:2] * spread_u], axis=0)
        tile = lax.dot_general(
            left.astype(jnp.bfloat16),
            spread_v.astype(jnp.bfloat16),
            (((1,), (1,)), ((), ())),
            preferred_element_type=jnp.float32,
        ).astype(jnp.bfloat16)
        out_ref[b] = jnp.concatenate([tile[:TU], tile[TU:]], axis=1)
        return carry

    lax.fori_loop(0, blocks, one, 0, unroll=4)
    out_ref[blocks] = ids_ref[...]


def column_kernel(meta_ref, band_ref, col_ref, tile_ref, table_ref, phase_ref, out_ref, acc_ref):
    step = pl.program_id(0)
    blocks = tile_ref.shape[1] - 1
    width = phase_ref.shape[1]
    chunk = 16

    @pl.when(step == 0)
    def _():
        acc_ref[...] = jnp.zeros_like(acc_ref)

    def some(q, carry):
        tiles = tile_ref[0, pl.ds(q * chunk, chunk)].reshape(chunk * TU, 2 * TV)
        cols = jnp.dot(tiles, table_ref[0], preferred_element_type=jnp.float32)
        for k in range(chunk):
            at = step * blocks + q * chunk + k
            band = band_ref[at]
            col = col_ref[at]
            cos = phase_ref[pl.ds(2 * col, 1), :]
            sin = phase_ref[pl.ds(2 * col + 1, 1), :]
            real = cols[k * TU : (k + 1) * TU, :width]
            imag = cols[k * TU : (k + 1) * TU, width:]
            rows = pl.ds(pl.multiple_of(band * TU, TU), TU)
            sum_real = real * cos - imag * sin
            sum_imag = real * sin + imag * cos
            for s in range(width // 128):
                acc_ref[s, rows, :] += sum_real[:, s * 128 : (s + 1) * 128]
                acc_ref[width // 128 + s, rows, :] += sum_imag[:, s * 128 : (s + 1) * 128]
        return carry

    lax.fori_loop(0, blocks // chunk, some, 0)

    @pl.when(step == pl.num_programs(0) - 1)
    def _():
        for i in range(TU):
            for s in range(2 * width // 128):
                part, at = divmod(s * 128, width)
                rows = acc_ref[s, pl.ds(i, BANDS, stride=TU), :]
                out_ref[i, pl.ds(part * BANDS, BANDS), pl.ds(at, 128)] = rows.astype(jnp.bfloat16)


def row_kernel(x_ref, band_ref, inner_ref, out_ref, mid_ref):
    width = x_ref.shape[2]

    def first(i, carry):
        y = jnp.dot(band_ref[...], x_ref[i], preferred_element_type=jnp.float32)
        mid_ref[pl.ds(2 * i, 2)] = y.astype(jnp.bfloat16).reshape(2, BANDS, width)
        return carry

    lax.fori_loop(0, TU, first, 0)

    def second(g, carry):
        rows = pl.ds(pl.multiple_of(g * 16, 16), 16)
        y = mid_ref[:, rows, :].reshape(2 * TU * 16, width)
        z = jnp.dot(inner_ref[g], y, preferred_element_type=jnp.float32)
        out_ref[:, rows, :] = z.astype(jnp.bfloat16).reshape(TU, 16, width)
        return carry

    lax.fori_loop(0, BANDS // 16, second, 0)


def shards(
    vis_values, kernel_u, kernel_v, offset_u, offset_v, block_owner, tile_slot, channel_freq
):
    row_count = lax.axis_size("row")
    freq_count = lax.axis_size("freq")
    blocks = vis_values.shape[1]
    vis_count = vis_values.shape[3]
    width = GRID // row_count
    tiles_slab = GRID // row_count // TU * TILE_COLS
    vmem = pl.BlockSpec(memory_space=pltpu.VMEM)
    params = pltpu.CompilerParams(vmem_limit_bytes=VMEM_LIMIT)

    freqs = lax.all_gather(channel_freq[0], "freq")
    tile = block_owner[0, :, 0] * tiles_slab + tile_slot[0]
    ids = jnp.stack([tile // TILE_COLS, tile % TILE_COLS]).astype(jnp.bfloat16)
    ids = jnp.pad(ids, ((0, TU - 2), (0, 2 * TV - blocks)))
    with jax.named_scope("gridding"):
        tiles = pl.pallas_call(
            grid_kernel,
            out_shape=jax.ShapeDtypeStruct((blocks + 1, TU, 2 * TV), jnp.bfloat16),
            in_specs=[vmem] * 6,
            out_specs=vmem,
            compiler_params=params,
        )(vis_values[0], kernel_u[0], kernel_v[0], offset_u[0], offset_v[0], ids)
    tiles = lax.all_gather(tiles, "row")
    ids = tiles[:, blocks, :2, :blocks].astype(jnp.int32)
    meta = lax.axis_index("row").astype(jnp.int32).reshape(1)
    with jax.named_scope("columns"):
        spectrum = pl.pallas_call(
            column_kernel,
            out_shape=jax.ShapeDtypeStruct((TU, 2 * BANDS, width), jnp.bfloat16),
            grid_spec=pltpu.PrefetchScalarGridSpec(
                num_scalar_prefetch=3,
                grid=(row_count,),
                in_specs=[
                    pl.BlockSpec((1, blocks + 1, TU, 2 * TV), lambda g, *_: (g, 0, 0, 0)),
                    pl.BlockSpec((1, 2 * TV, 2 * width), lambda g, meta, *_: (meta[0], 0, 0)),
                    pl.BlockSpec((2 * TILE_COLS, width), lambda g, *_: (0, 0)),
                ],
                out_specs=pl.BlockSpec((TU, 2 * BANDS, width), lambda g, *_: (0, 0, 0)),
                scratch_shapes=[pltpu.VMEM((2 * width // 128, GRID, 128), jnp.float32)],
            ),
            compiler_params=params,
        )(
            meta,
            ids[:, 0].reshape(-1),
            ids[:, 1].reshape(-1),
            tiles,
            tile_tables(row_count),
            phase_table(width),
        )
    scale = 1.0 / math.sqrt(blocks * row_count * vis_count)
    with jax.named_scope("rows"):
        dirty = pl.pallas_call(
            row_kernel,
            out_shape=jax.ShapeDtypeStruct((TU, BANDS, width), jnp.bfloat16),
            in_specs=[vmem] * 3,
            out_specs=vmem,
            scratch_shapes=[pltpu.VMEM((2 * TU, BANDS, width), jnp.bfloat16)],
            compiler_params=params,
        )(spectrum, band_table(scale), inner_table())
    dirty = dirty.reshape(freq_count, GRID // freq_count, width)
    dirty = lax.all_to_all(dirty, "freq", split_axis=0, concat_axis=0, tiled=True)
    x = (freqs - 1.284) / 0.428
    weights = jnp.stack([jnp.ones_like(x), x, x * x])
    outs = []
    for k in range(3):
        total = jnp.zeros(dirty.shape[1:], jnp.float32)
        for c in range(freq_count):
            total = total + (weights[k, c] * dirty[c].astype(jnp.float32))
        outs.append(total.astype(jnp.bfloat16))
    return jnp.stack(outs)


def solution(mesh):
    return jax.shard_map(
        shards,
        mesh=mesh,
        in_specs=(
            P("freq", "row", None, None),
            P("freq", "row", None, None),
            P("freq", "row", None, None),
            P("freq", "row", None),
            P("freq", "row", None),
            P("freq", "row", None),
            P("freq", "row"),
            P("freq"),
        ),
        out_specs=P(None, "freq", "row"),
        check_vma=False,
    )
```

time: 795 us -> 225 us (0.28); the launches traced: 785 us -> 225 us
  matrix products: 294 us -> 0 us
  waiting for transfers between devices: 319 us -> 38.2 us
  blocking collectives: 0 us -> 92.6 us
  local copies, waits for them, and re-layouts: 88.3 us -> 5.34 us
  Pallas kernels: 0 us -> 54.2 us
  other arithmetic: 51.5 us -> 15.1 us
  starting transfers between devices: 17.1 us -> 5.46 us
    dot_general x15 -> x0, matrix products: 294 us -> none  [the longest x1 109 us: grid_blocks(): jnp.einsum('spin,snj->spij', left, spread_v, preferred_element_type=jnp.f...]
    reduce_scatter x1 -> x0, waiting for transfers between devices: 213 us -> none  [shards(): lax.psum_scatter(terms_all.astype(jnp.bfloat16), 'freq', scatter_dimensio...]
    all_to_all x4 -> x1, waiting for transfers between devices: 107 us -> 0.01 us  [shards(): lax.all_to_all(dirty, 'freq', split_axis=0, concat_axis=0, tiled=True)]
    unnamed x0 -> x1, blocking collectives: none -> 92.6 us
    pallas_call x0 -> x3, Pallas kernels: none -> 54.2 us  [the longest x1 29.3 us: shards(): pl.pallas_call(column_kernel, out_shape=jax.ShapeDtypeStruct((TU, 2 * BAN...]
    all_gather x0 -> x1, waiting for transfers between devices: none -> 38.2 us  [shards(): tiles = lax.all_gather(tiles, 'row')]
    scatter-add x1 -> x0, other arithmetic: 30.5 us -> none  [shards(): slab_tiles = jnp.zeros((tiles_total, 2, TU, TV), jnp.float32).at[recv_til...]
    slice x4 -> x2, local copies, waits for them, and re-layouts: 24.2 us -> 0.69 us  [the longest x1 0.67 us: shards(): total = total + weights[k, c] * dirty[c].astype(jnp.float32)]
  transfers between devices with their start and end apart: 5 -> 2, of which waited for: 3 -> 1; matrix products, arithmetic and copies ran while one was open for 3% -> 1% of each run, Pallas kernels for 0% -> 0%
where the time goes in v1:
time: 225 us
  blocking collectives  92.6 us (41%)
  Pallas kernels  54.2 us (24%)
  waiting for transfers between devices  38.2 us (17%)
  other arithmetic  15.1 us (7%)
  between operations  14.1 us (6%)
  starting transfers between devices  5.46 us (2%)
  local copies, waits for them, and re-layouts  5.34 us (2%)
    unnamed x1, blocking collectives  92.6 us
    all_gather x1, waiting for transfers between devices, shards(): tiles = lax.all_gather(tiles, 'row')  38.2 us
    pallas_call x1, Pallas kernels, shards(): pl.pallas_call(column_kernel, out_shape=jax.ShapeDtypeStruct((TU, 2 * BAN...  29.3 us
    pallas_call x1, Pallas kernels, shards(): pl.pallas_call(row_kernel, out_shape=jax.ShapeDtypeStruct((TU, BANDS, wid...  18.6 us
    convert_element_type x2, other arithmetic, shards(): outs.append(total.astype(jnp.bfloat16))  11 us
    pallas_call x1, Pallas kernels, shards(): pl.pallas_call(grid_kernel, out_shape=jax.ShapeDtypeStruct((blocks + 1, T...  6.32 us
    all_to_all x1, starting transfers between devices, shards(): lax.all_to_all(dirty, 'freq', split_axis=0, concat_axis=0, tiled=True)  5.46 us
  transfers between devices with their start and end apart: 2, of which 1 were waited for; matrix products, arithmetic and copies ran while one was open for 1% of the time, Pallas kernels for 0%

profile of v1, /device:TPU:16, one launch (start us, length us, event | category | flops | bytes accessed | tf_op | source)
XLA Modules:
  0.0 225.0 jit_solution(14101544539270769841)
XLA Ops:
  6.5 0.0 all-gather.3.cloned.1.call-start
  6.5 0.7 fusion.17
  7.2 0.6 fusion.14.ids_ref
  7.8 1.8 copy_bitcast_fusion
  9.6 6.3 %gridding.1 = bf16[65,16,256]{2,1,0:T(8,128)(2,1)} custom-call(bf16[64,2,128]{2,1,0:T(2,128)(2,1)} %bitcast.38, bf16[64,7,128]{2,1,0:T(8,128)(2,1)} %get-tuple-element.26.ku_ref, bf16[64,7,128]{2,1,0:T(8,128)(2,1)} %get-tuple-element.25.kv_ref, s32[64,128]{1,0:T(8,128)} %bitcast.39, s32[64,128]{1,0:T(8,128)} %bitcast.40, bf16[16,256]{1,0:T(8,128)(2,1)} %fusion.14.ids_ref), custom_call_target="tpu_custom_call" | custom-call | tf_op jit(solution)/shard_map/gridding/pallas_call | solution.py:166
  16.0 0.0 all-gather.3.cloned.1.call-update
  16.0 38.2 %all-gather.3.cloned.1.call-done = bf16[520,16,256]{2,1,0:T(8,128)(2,1)} async-done(((bf16[65,16,256]{2,1,0:T(8,128)(2,1)}), bf16[520,16,256]{2,1,0:T(8,128)(2,1)}) %all-gather.3.cloned.1.call-update) | async-done | bytes 4259856 | tf_op jit(solution)/shard_map/all_gather | solution.py:173
  54.2 0.7 fusion.15
  55.0 0.7 squeeze.65.band_ref
  55.6 0.7 squeeze.66.col_ref
  56.3 29.3 %columns.1.x_ref = bf16[16,512,512]{2,1,0:T(8,128)(2,1)} custom-call(s32[1]{0:T(128)} %bitcast.meta_ref, s32[512]{0:T(512)} %squeeze.65.band_ref, s32[512]{0:T(512)} %squeeze.66.col_ref, bf16[8,65,16,256]{3,2,1,0:T(8,128)(2,1)} %bitcast.37, bf16[8,256,1024]{2,1,0:T(8,128)(2,1)} %constant.51.clone.table_ref, f32[64,512]{1,0:T(8,128)} %constant.52.clone.phase_ref), custom_call_target="tpu_custom_call" | custom-call | tf_op jit(solution)/shard_map/columns/pallas_call | solution.py:177
  85.5 18.6 %rows.1 = bf16[16,256,512]{2,1,0:T(8,128)(2,1)} custom-call(bf16[16,512,512]{2,1,0:T(8,128)(2,1)} %columns.1.x_ref, bf16[512,512]{1,0:T(8,128)(2,1)} %constant.53.clone.band_ref, bf16[16,256,512]{2,1,0:T(8,128)(2,1)} %constant.54.clone.inner_ref), custom_call_target="tpu_custom_call" | custom-call | tf_op jit(solution)/shard_map/rows/pallas_call | solution.py:202
  104.1 0.0 copy-start
  104.1 5.5 %all-to-all-start = ((bf16[4,1024,512]{2,1,0:T(8,128)(2,1)}), bf16[4,1024,512]{2,1,0:T(8,128)(2,1)}, u32[]{:S(2)}, u32[]{:S(2)}) async-start(bf16[4,1024,512]{2,1,0:T(8,128)(2,1)} %bitcast.35), calls=%async_computation | async-start | bytes 8388608 | tf_op jit(solution)/shard_map/all_to_all | solution.py:211
  110.3 0.0 copy-done
  110.3 0.6 dynamic-slice
  110.9 0.9 dynamic-update-slice
  111.8 92.6 %all-reduce.1 = f32[4]{0:T(128)S(1)} all-reduce(f32[4]{0:T(128)S(1)} %dynamic-update-slice), channel_id=1, replica_groups=mesh['freq'=4,'row'=8] {'freq'}, use_global_device_ids=true, to_apply=%add.1 | all-reduce | flops 4 | bytes 32
  204.4 0.7 fusion.19
  205.1 0.0 all-to-all-done
  205.1 5.6 %fusion.8 = (bf16[1,1024,512]{2,1,0:T(8,128)(2,1)S(1)}, bf16[1,1024,512]{2,1,0:T(8,128)(2,1)S(1)}) fusion(bf16[4,1024,512]{2,1,0:T(8,128)(2,1)} %all-to-all-done, f32[]{:T(128)} %bitcast.21, f32[]{:T(128)} %bitcast.20, f32[]{:T(128)} %bitcast.19, f32[]{:T(128)} %bitcast.18), kind=kLoop, calls=%fused_computation.20 | loop fusion | flops 8388608 | bytes 6291472 | tf_op jit(solution)/shard_map/convert_element_type | solution.py:219
  210.7 5.4 %fusion.3 = bf16[1,1024,512]{2,1,0:T(8,128)(2,1)S(1)} fusion(f32[]{:T(128)} %bitcast.16, f32[]{:T(128)} %bitcast.15, f32[]{:T(128)} %bitcast.14, f32[]{:T(128)} %bitcast.13, bf16[4,1024,512]{2,1,0:T(8,128)(2,1)} %all-to-all-done), kind=kLoop, calls=%fused_computation.15 | loop fusion | flops 6291456 | bytes 5242896 | tf_op jit(solution)/shard_map/convert_element_type | solution.py:219
  216.1 2.0 pad_maximum_fusion
  (4 shorter events, 0.0 us)
Async XLA Ops:
  6.5 47.7 %all-gather.3.cloned.1.call-start = ((), (), s32[]{:S(2)}) async-start(), calls=%async_computation.1 | async-start | bytes 4792320 | tf_op jit(solution)/shard_map/all_gather | solution.py:173
  104.1 6.1 %copy-start = (u32[32]{0:T(128)S(1)}, u32[32]{0:T(128)}, u32[]{:S(2)}) copy-start(u32[32]{0:T(128)} %constant.67) | copy-start | bytes 388
  104.1 101.0 %all-to-all-start = ((bf16[4,1024,512]{2,1,0:T(8,128)(2,1)}), bf16[4,1024,512]{2,1,0:T(8,128)(2,1)}, u32[]{:S(2)}, u32[]{:S(2)}) async-start(bf16[4,1024,512]{2,1,0:T(8,128)(2,1)} %bitcast.35), calls=%async_computation | async-start | bytes 8388608 | tf_op jit(solution)/shard_map/all_to_all | solution.py:211
Sparse Core Ops, SparseCore 0:
  16.1 38.0 all-gather.2

commit v2 on v1

v2 whole, which is shorter than its diff:
```python
from functools import partial
import math

import jax
import jax.numpy as jnp
import ml_dtypes
import numpy as np
from jax import lax
from jax.experimental import pallas as pl
from jax.experimental.pallas import tpu as pltpu
from jax.sharding import PartitionSpec as P

GRID = 4096
TU = 16
TV = 128
BANDS = GRID // TU
TILE_COLS = GRID // TV
BF16 = ml_dtypes.bfloat16
VMEM_LIMIT = 56 * 1024 * 1024


def turn(index, length):
    angle = 2.0 * np.pi * (index % length) / length
    return np.cos(angle), np.sin(angle)


def tile_tables(row_count, chunk):
    j = np.arange(TV)[:, None]
    m = np.arange(GRID)[None, :]
    cos, sin = turn(j * m, GRID)
    cos = cos.reshape(TV, row_count, -1, chunk).transpose(1, 2, 0, 3)
    sin = sin.reshape(TV, row_count, -1, chunk).transpose(1, 2, 0, 3)
    top = np.concatenate([cos, sin], axis=3)
    low = np.concatenate([-sin, cos], axis=3)
    return np.concatenate([top, low], axis=2).astype(BF16)


def phase_table(chunk):
    cos, sin = turn(np.arange(TILE_COLS)[:, None] * np.arange(chunk)[None, :], TILE_COLS)
    whole = np.concatenate([cos, sin], axis=1).astype(np.float32)
    main = whole.astype(BF16)
    return np.concatenate([main, (whole - main.astype(np.float32)).astype(BF16)], axis=0)


def band_table(scale):
    index = np.arange(BANDS)
    cos, sin = turn(index[:, None] * index[None, :], BANDS)
    return (np.concatenate([cos, sin], axis=0) * scale).astype(BF16)


def inner_table():
    groups = BANDS // 16
    g = np.arange(groups)[:, None, None, None]
    high = np.arange(TU)[None, :, None, None]
    low = np.arange(16)[None, None, :, None]
    i = np.arange(TU)[None, None, None, :]
    cos, sin = turn(i * (16 * g + low + BANDS * high), GRID)
    parts = np.stack([cos, -sin], axis=4)
    full = parts[..., None] * np.eye(16)[None, None, :, None, None, :]
    return full.reshape(groups, TU * 16, TU * 2 * 16).astype(BF16)


def grid_kernel(vis_ref, ku_ref, kv_ref, ou_ref, ov_ref, ids_ref, out_ref, tile_ref):
    blocks, taps = ku_ref.shape[0], ku_ref.shape[1]

    def one(b, carry):
        d_u = lax.broadcasted_iota(jnp.int32, (TU, TV), 0) - ou_ref[pl.ds(b, 1), :]
        d_v = lax.broadcasted_iota(jnp.int32, (TV, TV), 0) - ov_ref[pl.ds(b, 1), :]
        ku = ku_ref[b].astype(jnp.float32)
        kv = kv_ref[b].astype(jnp.float32)
        vis = vis_ref[b].astype(jnp.float32)
        spread_u = jnp.zeros((TU, TV), jnp.float32)
        spread_v = jnp.zeros((TV, TV), jnp.float32)
        for t in range(taps):
            spread_u = jnp.where(d_u == t, ku[t : t + 1], spread_u)
            spread_v = jnp.where(d_v == t, kv[t : t + 1], spread_v)
        left = jnp.concatenate([vis[0:1] * spread_u, vis[1:2] * spread_u], axis=0)
        tile = lax.dot_general(
            left.astype(jnp.bfloat16),
            spread_v.astype(jnp.bfloat16),
            (((1,), (1,)), ((), ())),
            preferred_element_type=jnp.float32,
        )
        for i in range(TU):
            tile_ref[i, pl.ds(b, 1), :] = tile[i : i + 1]
            tile_ref[TU + i, pl.ds(b, 1), :] = tile[TU + i : TU + i + 1]
        return carry

    lax.fori_loop(0, blocks, one, 0, unroll=4)
    out_ref[:TU, :, :TV] = tile_ref[:TU].astype(jnp.bfloat16)
    out_ref[:TU, :, TV:] = tile_ref[TU:].astype(jnp.bfloat16)
    out_ref[TU] = ids_ref[...]


def image_kernel(
    freq_count,
    tiles_ref,
    band_ref,
    col_ref,
    x_ref,
    tile_table_ref,
    phase_table_ref,
    band_table_ref,
    inner_ref,
    out_ref,
    factor_ref,
    phase_ref,
    mid_ref,
    send_ref,
    recv_ref,
    x_recv_ref,
    send_sem,
    recv_sem,
    x_send_sem,
    x_recv_sem,
):
    me = lax.axis_index("freq")
    blocks = tiles_ref.shape[0] * tiles_ref.shape[2]
    chunks, chunk = send_ref.shape[0], send_ref.shape[3]
    share = TU // freq_count
    half = freq_count // 2
    shifts = sorted(range(1, freq_count), key=lambda d: abs(d - half))
    peers = [lax.rem(me + d, freq_count) for d in shifts]

    barrier = pltpu.get_barrier_semaphore()
    for peer in peers:
        pl.semaphore_signal(
            barrier, inc=1, device_id={"freq": peer}, device_id_type=pl.DeviceIdType.MESH
        )

    bands = lax.broadcasted_iota(jnp.int32, (BANDS, blocks), 0) == band_ref[...]
    picked = jnp.dot(
        band_table_ref[...],
        bands.astype(jnp.float32).astype(jnp.bfloat16),
        preferred_element_type=jnp.float32,
    ).astype(jnp.bfloat16)
    factor_ref[:BANDS, :blocks] = picked[:BANDS]
    factor_ref[:BANDS, blocks:] = -picked[BANDS:]
    factor_ref[BANDS:, :blocks] = picked[BANDS:]
    factor_ref[BANDS:, blocks:] = picked[:BANDS]
    at = lax.broadcasted_iota(jnp.int32, (2 * TILE_COLS, blocks), 0)
    cols = (at == col_ref[...]) | (at == col_ref[...] + TILE_COLS)
    phase_ref[...] = lax.dot_general(
        cols.astype(jnp.float32).astype(jnp.bfloat16),
        phase_table_ref[...],
        (((0,), (0,)), ((), ())),
        preferred_element_type=jnp.float32,
    )

    copies = []
    for q in range(chunks):

        def first(i, carry):
            tiles = tiles_ref[:, pl.ds(i, 1)].reshape(blocks, 2 * TV)
            cols = jnp.dot(tiles, tile_table_ref[q], preferred_element_type=jnp.float32)
            real, imag = cols[:, :chunk], cols[:, chunk:]
            cos, sin = phase_ref[:, :chunk], phase_ref[:, chunk:]
            turned = jnp.concatenate(
                [
                    (real * cos - imag * sin).astype(jnp.bfloat16),
                    (real * sin + imag * cos).astype(jnp.bfloat16),
                ],
                axis=0,
            )
            y = jnp.dot(factor_ref[...], turned, preferred_element_type=jnp.float32)
            mid_ref[pl.ds(2 * i, 2)] = y.astype(jnp.bfloat16).reshape(2, BANDS, chunk)
            return carry

        lax.fori_loop(0, TU, first, 0)

        def second(g, carry):
            rows = pl.ds(pl.multiple_of(g * 16, 16), 16)
            y = mid_ref[:, rows, :].reshape(2 * TU * 16, chunk)
            z = jnp.dot(inner_ref[g], y, preferred_element_type=jnp.float32)
            send_ref[q, :, rows, :] = z.astype(jnp.bfloat16).reshape(TU, 16, chunk)
            return carry

        lax.fori_loop(0, BANDS // 16, second, 0)

        if q == 0:
            pl.semaphore_wait(barrier, freq_count - 1)
            for s, peer in enumerate(peers):
                copy = pltpu.make_async_remote_copy(
                    src_ref=x_ref,
                    dst_ref=x_recv_ref.at[s],
                    send_sem=x_send_sem.at[s],
                    recv_sem=x_recv_sem.at[s],
                    device_id={"freq": peer},
                    device_id_type=pl.DeviceIdType.MESH,
                )
                copy.start()
                copies.append(copy)
        for s, peer in enumerate(peers):
            copy = pltpu.make_async_remote_copy(
                src_ref=send_ref.at[q, pl.ds(peer * share, share)],
                dst_ref=recv_ref.at[q, s],
                send_sem=send_sem.at[q, s],
                recv_sem=recv_sem.at[q, s],
                device_id={"freq": peer},
                device_id_type=pl.DeviceIdType.MESH,
            )
            copy.start()
            copies.append(copy)

    own = x_ref[0:1, :]
    for copy in copies[: freq_count - 1]:
        copy.wait()
    others = [x_recv_ref[s, 0:1, :] for s in range(freq_count - 1)]
    step = 32
    for q in range(chunks):
        for s in range(freq_count - 1):
            copies[(q + 1) * (freq_count - 1) + s].wait()

        def combine(at, carry):
            h = at // (BANDS // step)
            rows = pl.ds(pl.multiple_of(at % (BANDS // step) * step, step), step)
            image = send_ref[q, me * share + h, rows, :].astype(jnp.float32)
            total = [image, own * image, (own * own) * image]
            for s in range(freq_count - 1):
                image = recv_ref[q, s, h, rows, :].astype(jnp.float32)
                x = others[s]
                total[0] += image
                total[1] += x * image
                total[2] += (x * x) * image
            for k in range(3):
                out_ref[k, h, rows, q * chunk : (q + 1) * chunk] = total[k].astype(jnp.bfloat16)
            return carry

        lax.fori_loop(0, share * (BANDS // step), combine, 0)


def shards(
    vis_values, kernel_u, kernel_v, offset_u, offset_v, block_owner, tile_slot, channel_freq
):
    row_count = lax.axis_size("row")
    freq_count = lax.axis_size("freq")
    blocks = vis_values.shape[1]
    vis_count = vis_values.shape[3]
    width = GRID // row_count
    tiles_slab = GRID // row_count // TU * TILE_COLS
    vmem = pl.BlockSpec(memory_space=pltpu.VMEM)
    params = pltpu.CompilerParams(vmem_limit_bytes=VMEM_LIMIT)

    chunk = min(256, width)
    chunks = width // chunk
    peers = freq_count - 1
    share = TU // freq_count

    tile = block_owner[0, :, 0] * tiles_slab + tile_slot[0]
    ids = jnp.stack([tile // TILE_COLS, tile % TILE_COLS]).astype(jnp.bfloat16)
    ids = jnp.pad(ids, ((0, blocks - 2), (0, 2 * TV - blocks)))
    with jax.named_scope("gridding"):
        tiles = pl.pallas_call(
            grid_kernel,
            out_shape=jax.ShapeDtypeStruct((TU + 1, blocks, 2 * TV), jnp.bfloat16),
            in_specs=[vmem] * 6,
            out_specs=vmem,
            scratch_shapes=[pltpu.VMEM((2 * TU, blocks, TV), jnp.float32)],
            compiler_params=params,
        )(vis_values[0], kernel_u[0], kernel_v[0], offset_u[0], offset_v[0], ids)
    tiles = lax.all_gather(tiles, "row")
    ids = tiles[:, TU, :2, :blocks].astype(jnp.int32)
    x = jnp.broadcast_to((channel_freq - 1.284) / 0.428, (8, chunk))
    table = lax.dynamic_index_in_dim(
        jnp.asarray(tile_tables(row_count, chunk)), lax.axis_index("row"), 0, keepdims=False
    )
    scale = 1.0 / math.sqrt(blocks * row_count * vis_count)
    total_blocks = row_count * blocks
    with jax.named_scope("image"):
        image = pl.pallas_call(
            partial(image_kernel, freq_count),
            out_shape=jax.ShapeDtypeStruct((3, share, BANDS, width), jnp.bfloat16),
            in_specs=[vmem] * 8,
            out_specs=vmem,
            scratch_shapes=[
                pltpu.VMEM((2 * BANDS, 2 * total_blocks), jnp.bfloat16),
                pltpu.VMEM((total_blocks, 2 * chunk), jnp.float32),
                pltpu.VMEM((2 * TU, BANDS, chunk), jnp.bfloat16),
                pltpu.VMEM((chunks, TU, BANDS, chunk), jnp.bfloat16),
                pltpu.VMEM((chunks, peers, share, BANDS, chunk), jnp.bfloat16),
                pltpu.VMEM((peers, 8, chunk), jnp.float32),
                pltpu.SemaphoreType.DMA((chunks, peers)),
                pltpu.SemaphoreType.DMA((chunks, peers)),
                pltpu.SemaphoreType.DMA((peers,)),
                pltpu.SemaphoreType.DMA((peers,)),
            ],
            compiler_params=pltpu.CompilerParams(
                vmem_limit_bytes=VMEM_LIMIT, collective_id=0, has_side_effects=True
            ),
        )(
            tiles,
            ids[:, 0].reshape(1, -1),
            ids[:, 1].reshape(1, -1),
            x,
            table,
            phase_table(chunk),
            band_table(scale),
            inner_table(),
        )
    return image.reshape(3, GRID // freq_count, width)


def solution(mesh):
    return jax.shard_map(
        shards,
        mesh=mesh,
        in_specs=(
            P("freq", "row", None, None),
            P("freq", "row", None, None),
            P("freq", "row", None, None),
            P("freq", "row", None),
            P("freq", "row", None),
            P("freq", "row", None),
            P("freq", "row"),
            P("freq"),
        ),
        out_specs=P(None, "freq", "row"),
        check_vma=False,
    )
```

time: 225 us -> 189 us (0.84)
  blocking collectives: 92.6 us -> 0 us
  Pallas kernels: 54.2 us -> 125 us
  other arithmetic: 15.1 us -> 2.03 us
  starting transfers between devices: 5.46 us -> 0.01 us
  local copies, waits for them, and re-layouts: 5.34 us -> 9.39 us
    unnamed x1 -> x0, blocking collectives: 92.6 us -> none
    pallas_call x3 -> x2, Pallas kernels: 54.2 us -> 125 us  [the longest x1 118 us: shards(): pl.pallas_call(partial(image_kernel, freq_count), out_shape=jax.ShapeDtyp...]
    convert_element_type x3 -> x1, other arithmetic: 11.8 us -> 0.72 us  [shards(): ids = tiles[:, TU, :2, :blocks].astype(jnp.int32)]
    all_to_all x1 -> x0, starting transfers between devices: 5.46 us -> none  [shards(): lax.all_to_all(dirty, 'freq', split_axis=0, concat_axis=0, tiled=True)]
  transfers between devices with their start and end apart: 2 -> 1, of which waited for: 1 -> 1; matrix products, arithmetic and copies ran while one was open for 1% -> 1% of each run, Pallas kernels for 0% -> 0%
where the time goes in v2:
time: 189 us; the launch traced here: 187 us
  Pallas kernels  125 us (66%)
  waiting for transfers between devices  36.5 us (19%)
  between operations  14.1 us (7%)
  local copies, waits for them, and re-layouts  9.39 us (5%)
  other arithmetic  2.03 us (1%)
    pallas_call x1, Pallas kernels, shards(): pl.pallas_call(partial(image_kernel, freq_count), out_shape=jax.ShapeDtyp...  118 us
    all_gather x1, waiting for transfers between devices, shards(): tiles = lax.all_gather(tiles, 'row')  36.5 us
    pallas_call x1, Pallas kernels, shards(): pl.pallas_call(grid_kernel, out_shape=jax.ShapeDtypeStruct((TU + 1, block...  6.78 us
  transfers between devices with their start and end apart: 1, of which 1 were waited for; matrix products, arithmetic and copies ran while one was open for 1% of the time, Pallas kernels for 0%

profile of v2, /device:TPU:16, one launch (start us, length us, event | category | flops | bytes accessed | tf_op | source)
XLA Modules:
  0.0 187.2 jit_solution(5312463779307481731)
XLA Ops:
  6.5 0.0 all-gather.3.cloned.1.call-start
  6.5 0.7 fusion.8
  7.2 0.6 fusion.5.ids_ref
  7.8 1.8 copy_bitcast_fusion
  9.7 6.8 %gridding.1 = bf16[17,64,256]{2,1,0:T(8,128)(2,1)} custom-call(bf16[64,2,128]{2,1,0:T(2,128)(2,1)} %bitcast.27, bf16[64,7,128]{2,1,0:T(8,128)(2,1)} %get-tuple-element.10.ku_ref, bf16[64,7,128]{2,1,0:T(8,128)(2,1)} %get-tuple-element.9.kv_ref, s32[64,128]{1,0:T(8,128)} %bitcast.28, s32[64,128]{1,0:T(8,128)} %bitcast.29, bf16[64,256]{1,0:T(8,128)(2,1)} %fusion.5.ids_ref), custom_call_target="tpu_custom_call" | custom-call | tf_op jit(solution)/shard_map/gridding/pallas_call | solution.py:253
  16.4 0.0 all-gather.3.cloned.1.call-update
  17.1 1.9 %dynamic-slice_bitcast_fusion.tile_table_ref = bf16[2,256,512]{2,1,0:T(8,128)(2,1)} fusion(bf16[8,2,256,512]{3,2,1,0:T(8,128)(2,1)} %constant.56.clone, s32[]{:T(128)S(6)} %select_n.20), kind=kLoop, calls=%fused_computation | loop fusion | bytes 1048580 | tf_op jit(solution)/shard_map/jit(dynamic_index_in_dim)/squeeze | solution.py:264
  19.0 36.5 %all-gather.3.cloned.1.call-done = bf16[136,64,256]{2,1,0:T(8,128)(2,1)} async-done(((bf16[17,64,256]{2,1,0:T(8,128)(2,1)}), bf16[136,64,256]{2,1,0:T(8,128)(2,1)}) %all-gather.3.cloned.1.call-update) | async-done | bytes 4456464 | tf_op jit(solution)/shard_map/all_gather | solution.py:261
  55.5 0.7 fusion.6
  56.2 0.7 squeeze.34.col_ref
  56.9 0.7 squeeze.33.band_ref
  57.6 0.6 broadcast_in_dim.2.x_ref
  58.2 118.5 %image.1 = bf16[3,4,256,512]{3,2,1,0:T(8,128)(2,1)} custom-call(bf16[8,17,64,256]{3,2,1,0:T(8,128)(2,1)} %bitcast.26, s32[1,512]{1,0:T(1,128)} %squeeze.33.band_ref, s32[1,512]{1,0:T(1,128)} %squeeze.34.col_ref, f32[8,256]{1,0:T(8,128)} %broadcast_in_dim.2.x_ref, bf16[2,256,512]{2,1,0:T(8,128)(2,1)} %dynamic-slice_bitcast_fusion.tile_table_ref, ...), custom_call_target="tpu_custom_call" | custom-call | tf_op jit(solution)/shard_map/image/pallas_call | solution.py:270
  176.6 3.8 %copy.21 = bf16[3,1024,512]{2,1,0:T(8,128)(2,1)} copy(bf16[3,1024,512]{2,1,0:T(8,128)(2,1)} %bitcast.24) | data formatting | bytes 6291456
  (2 shorter events, 0.0 us)
Async XLA Ops:
  6.5 49.0 %all-gather.3.cloned.1.call-start = ((), (), s32[]{:S(2)}) async-start(), calls=%async_computation | async-start | bytes 5013504 | tf_op jit(solution)/shard_map/all_gather | solution.py:261
Sparse Core Ops, SparseCore 0:
  16.6 38.8 all-gather.2

commit v3 on v2

v3 whole, which is shorter than its diff:
```python
from functools import partial
import math

import jax
import jax.numpy as jnp
import ml_dtypes
import numpy as np
from jax import lax
from jax.experimental import pallas as pl
from jax.experimental.pallas import tpu as pltpu
from jax.sharding import PartitionSpec as P

GRID = 4096
TU = 16
TV = 128
BANDS = GRID // TU
TILE_COLS = GRID // TV
BF16 = ml_dtypes.bfloat16
VMEM_LIMIT = 56 * 1024 * 1024


def turn(index, length):
    angle = 2.0 * np.pi * (index % length) / length
    return np.cos(angle), np.sin(angle)


def tile_tables(row_count, chunk):
    j = np.arange(TV)[:, None]
    m = np.arange(GRID)[None, :]
    cos, sin = turn(j * m, GRID)
    cos = cos.reshape(TV, row_count, -1, chunk).transpose(1, 2, 0, 3)
    sin = sin.reshape(TV, row_count, -1, chunk).transpose(1, 2, 0, 3)
    top = np.concatenate([cos, sin], axis=3)
    low = np.concatenate([-sin, cos], axis=3)
    return np.concatenate([top, low], axis=2).astype(BF16)


def phase_table(chunk):
    cos, sin = turn(np.arange(TILE_COLS)[:, None] * np.arange(chunk)[None, :], TILE_COLS)
    whole = np.concatenate([cos, sin], axis=1).astype(np.float32)
    main = whole.astype(BF16)
    return np.concatenate([main, (whole - main.astype(np.float32)).astype(BF16)], axis=0)


def band_table(scale):
    index = np.arange(BANDS)
    cos, sin = turn(index[:, None] * index[None, :], BANDS)
    return (np.concatenate([cos, sin], axis=0) * scale).astype(BF16)


def inner_table():
    groups = BANDS // 16
    g = np.arange(groups)[:, None, None, None]
    high = np.arange(TU)[None, :, None, None]
    low = np.arange(16)[None, None, :, None]
    i = np.arange(TU)[None, None, None, :]
    cos, sin = turn(i * (16 * g + low + BANDS * high), GRID)
    parts = np.stack([cos, -sin], axis=4)
    full = parts[..., None] * np.eye(16)[None, None, :, None, None, :]
    return full.reshape(groups, TU * 16, TU * 2 * 16).astype(BF16)


def grid_tiles(vis_ref, ku_ref, kv_ref, ou_ref, ov_ref, tile_ref):
    blocks, taps = ku_ref.shape[1], ku_ref.shape[2]

    def one(b, carry):
        d_u = lax.broadcasted_iota(jnp.int32, (TU, TV), 0) - ou_ref[0, pl.ds(b, 1), :]
        d_v = lax.broadcasted_iota(jnp.int32, (TV, TV), 0) - ov_ref[0, pl.ds(b, 1), :]
        ku = ku_ref[0, b].astype(jnp.float32)
        kv = kv_ref[0, b].astype(jnp.float32)
        vis = vis_ref[0, b].astype(jnp.float32)
        spread_u = jnp.zeros((TU, TV), jnp.float32)
        spread_v = jnp.zeros((TV, TV), jnp.float32)
        for t in range(taps):
            spread_u = jnp.where(d_u == t, ku[t : t + 1], spread_u)
            spread_v = jnp.where(d_v == t, kv[t : t + 1], spread_v)
        left = jnp.concatenate([vis[0:1] * spread_u, vis[1:2] * spread_u], axis=0)
        tile = lax.dot_general(
            left.astype(jnp.bfloat16),
            spread_v.astype(jnp.bfloat16),
            (((1,), (1,)), ((), ())),
            preferred_element_type=jnp.float32,
        )
        for i in range(TU):
            tile_ref[i, pl.ds(b, 1), :] = tile[i : i + 1]
            tile_ref[TU + i, pl.ds(b, 1), :] = tile[TU + i : TU + i + 1]
        return carry

    lax.fori_loop(0, blocks, one, 0, unroll=4)


def image_kernel(
    freq_count,
    row_count,
    vis_ref,
    ku_ref,
    kv_ref,
    ou_ref,
    ov_ref,
    ids_ref,
    x_ref,
    phase_table_ref,
    band_table_ref,
    tile_table_hbm,
    inner_hbm,
    out_ref,
    grid_ref,
    tiles_ref,
    tile_table_ref,
    inner_ref,
    factor_ref,
    phase_ref,
    mid_ref,
    send_ref,
    recv_ref,
    x_send_ref,
    x_recv_ref,
    table_sem,
    swap_sem,
    row_send,
    row_recv,
    core_send,
    core_recv,
    send_sem,
    recv_sem,
    x_send_sem,
    x_recv_sem,
):
    me, row = lax.axis_index("freq"), lax.axis_index("row")
    block_count = ku_ref.shape[1]
    blocks = row_count * block_count
    chunks, chunk = send_ref.shape[1], send_ref.shape[4]
    share = TU // freq_count
    half = freq_count // 2
    first_of_half = me // half * half
    partner = lax.rem(me + half, freq_count)
    group = [first_of_half + lax.rem(me - first_of_half + d, half) for d in range(1, half)]
    pairs = row_count // 2
    pair, sub = row // 2, lax.rem(row, 2)
    sibling = pair * 2 + 1 - sub
    targets = [lax.rem(pair + d, pairs) * 2 + sub for d in range(1, pairs)]
    sources = [lax.rem(pair + pairs - d, pairs) * 2 + sub for d in range(1, pairs)]
    everyone = [{"freq": f} for f in [partner] + group] + [{"row": r} for r in [sibling] + targets]

    barrier = pltpu.get_barrier_semaphore()
    for device in everyone:
        pl.semaphore_signal(
            barrier, inc=1, device_id=device, device_id_type=pl.DeviceIdType.MESH
        )
    inner_rows = pl.ds(first_of_half * share * 16, TU // 2 * 16)
    tables = [
        pltpu.make_async_copy(tile_table_hbm.at[row], tile_table_ref, table_sem.at[0]),
        pltpu.make_async_copy(inner_hbm.at[:, inner_rows, :], inner_ref, table_sem.at[1]),
    ]
    for copy in tables:
        copy.start()

    grid_tiles(vis_ref, ku_ref, kv_ref, ou_ref, ov_ref, grid_ref)
    for i in range(TU):
        rows = slice(i * block_count, (i + 1) * block_count)
        tiles_ref[0, row, rows, :TV] = grid_ref[i].astype(jnp.bfloat16)
        tiles_ref[0, row, rows, TV:] = grid_ref[TU + i].astype(jnp.bfloat16)
    meta_rows = slice(TU * block_count, TU * block_count + 16)
    x = x_ref[...]
    x_main = x.astype(jnp.bfloat16).astype(jnp.float32)
    x_next = (x - x_main).astype(jnp.bfloat16).astype(jnp.float32)
    x_last = x - x_main - x_next
    line = lax.broadcasted_iota(jnp.int32, (16, 2 * TV), 0)
    meta = jnp.where(line == 2, x_main, ids_ref[...])
    meta = jnp.where(line == 3, x_next, jnp.where(line == 4, x_last, meta))
    tiles_ref[0, row, meta_rows, :] = meta.astype(jnp.bfloat16)

    def remote(src, dst, send, recv, device):
        copy = pltpu.make_async_remote_copy(
            src_ref=src,
            dst_ref=dst,
            send_sem=send,
            recv_sem=recv,
            device_id=device,
            device_id_type=pl.DeviceIdType.MESH,
        )
        copy.start()
        return copy

    def to_rows(c):
        own = tiles_ref.at[c, row]
        direct = [
            remote(own, own, row_send.at[c, n], row_recv.at[c, n], {"row": target})
            for n, target in enumerate(targets)
        ]
        return direct, [
            remote(own, own, core_send.at[c, 0], core_recv.at[c, 0], {"row": sibling})
        ]

    def forward(c, direct):
        passed = []
        for n, source in enumerate(sources):
            direct[n].wait_recv()
            block = tiles_ref.at[c, source]
            passed.append(
                remote(
                    block,
                    block,
                    core_send.at[c, n + 1],
                    core_recv.at[c, n + 1],
                    {"row": sibling},
                )
            )
        return passed

    pl.semaphore_wait(barrier, len(everyone))
    swap = remote(
        tiles_ref.at[0, row],
        tiles_ref.at[1, row],
        swap_sem.at[0],
        swap_sem.at[1],
        {"freq": partner},
    )
    direct_a, near_a = to_rows(0)
    near_a += forward(0, direct_a)
    swap.wait_recv()
    direct_b, near_b = to_rows(1)

    def x_of(c):
        meta = tiles_ref[c, row, meta_rows, :].astype(jnp.float32)
        return meta[2:3] + (meta[3:4] + meta[4:5])

    x_own = [x_of(0)[:, :chunk], x_of(1)[:, :chunk]]
    for c in range(2):
        x_send_ref[c * 8 : (c + 1) * 8, :] = jnp.broadcast_to(x_own[c], (8, chunk))
    x_copies = [
        remote(x_send_ref, x_recv_ref.at[n], x_send_sem.at[n], x_recv_sem.at[n], {"freq": peer})
        for n, peer in enumerate(group)
    ]
    for copy in near_a:
        copy.wait_recv()
    for copy in tables:
        copy.wait()

    def channel(c):
        for p in range(pairs):
            at = meta_rows.start
            ids = (
                tiles_ref[c, 2 * p, at : at + 16, :TV].astype(jnp.float32)
                + tiles_ref[c, 2 * p + 1, at : at + 16, :TV].astype(jnp.float32)
            )
            ids = ids.astype(jnp.int32)
            lanes = slice(p * TV, (p + 1) * TV)
            bands = lax.broadcasted_iota(jnp.int32, (BANDS, TV), 0) == ids[0:1]
            picked = jnp.dot(
                band_table_ref[...],
                bands.astype(jnp.float32).astype(jnp.bfloat16),
                preferred_element_type=jnp.float32,
            ).astype(jnp.bfloat16)
            imag_lanes = slice(blocks + p * TV, blocks + (p + 1) * TV)
            factor_ref[:BANDS, lanes] = picked[:BANDS]
            factor_ref[:BANDS, imag_lanes] = -picked[BANDS:]
            factor_ref[BANDS:, lanes] = picked[BANDS:]
            factor_ref[BANDS:, imag_lanes] = picked[:BANDS]
            at = lax.broadcasted_iota(jnp.int32, (2 * TILE_COLS, TV), 0)
            cols = (at == ids[1:2]) | (at == ids[1:2] + TILE_COLS)
            phase_ref[lanes, :] = lax.dot_general(
                cols.astype(jnp.float32).astype(jnp.bfloat16),
                phase_table_ref[...],
                (((0,), (0,)), ((), ())),
                preferred_element_type=jnp.float32,
            )

        copies = []
        for q in range(chunks):

            def first(i, carry):
                rows = pl.ds(pl.multiple_of(i * block_count, block_count), block_count)
                tiles = tiles_ref[c, :, rows, :].reshape(blocks, 2 * TV)
                cols = jnp.dot(tiles, tile_table_ref[q], preferred_element_type=jnp.float32)
                real, imag = cols[:, :chunk], cols[:, chunk:]
                cos, sin = phase_ref[:, :chunk], phase_ref[:, chunk:]
                turned = jnp.concatenate(
                    [
                        (real * cos - imag * sin).astype(jnp.bfloat16),
                        (real * sin + imag * cos).astype(jnp.bfloat16),
                    ],
                    axis=0,
                )
                y = jnp.dot(factor_ref[...], turned, preferred_element_type=jnp.float32)
                mid_ref[pl.ds(2 * i, 2)] = y.astype(jnp.bfloat16).reshape(2, BANDS, chunk)
                return carry

            lax.fori_loop(0, TU, first, 0)

            def second(g, carry):
                rows = pl.ds(pl.multiple_of(g * 16, 16), 16)
                y = mid_ref[:, rows, :].reshape(2 * TU * 16, chunk)
                z = jnp.dot(inner_ref[g], y, preferred_element_type=jnp.float32)
                send_ref[c, q, :, rows, :] = z.astype(jnp.bfloat16).reshape(TU // 2, 16, chunk)
                return carry

            lax.fori_loop(0, BANDS // 16, second, 0)
            for n, peer in enumerate(group):
                copies.append(
                    remote(
                        send_ref.at[c, q, pl.ds((peer - first_of_half) * share, share)],
                        recv_ref.at[c, q, n],
                        send_sem.at[c, q, n],
                        recv_sem.at[c, q, n],
                        {"freq": peer},
                    )
                )
        return copies

    images = channel(0)
    near_b += forward(1, direct_b)
    for copy in near_b:
        copy.wait_recv()
    images += channel(1)

    for copy in x_copies:
        copy.wait()
    for copy in direct_a + direct_b + near_a + near_b + [swap]:
        copy.wait_send()
    step = 32
    for q in range(chunks):
        for c in range(2):
            for n in range(half - 1):
                images[(c * chunks + q) * (half - 1) + n].wait()

        def combine(at, carry):
            h = at // (BANDS // step)
            rows = pl.ds(pl.multiple_of(at % (BANDS // step) * step, step), step)
            total = [jnp.zeros((step, chunk), jnp.float32) for _ in range(3)]
            for c in range(2):
                own_at = (me - first_of_half) * share + h
                terms = [(x_own[c], send_ref[c, q, own_at, rows, :])]
                for n in range(half - 1):
                    x_other = x_recv_ref[n, c * 8 : c * 8 + 1, :]
                    terms.append((x_other, recv_ref[c, q, n, h, rows, :]))
                for x_term, image in terms:
                    image = image.astype(jnp.float32)
                    total[0] += image
                    total[1] += x_term * image
                    total[2] += (x_term * x_term) * image
            for k in range(3):
                out_ref[k, h, rows, q * chunk : (q + 1) * chunk] = total[k].astype(jnp.bfloat16)
            return carry

        lax.fori_loop(0, share * (BANDS // step), combine, 0)


def shards(
    vis_values, kernel_u, kernel_v, offset_u, offset_v, block_owner, tile_slot, channel_freq
):
    row_count = lax.axis_size("row")
    freq_count = lax.axis_size("freq")
    blocks = vis_values.shape[1]
    vis_count = vis_values.shape[3]
    width = GRID // row_count
    tiles_slab = GRID // row_count // TU * TILE_COLS
    vmem = pl.BlockSpec(memory_space=pltpu.VMEM)
    chunk = min(256, width)
    chunks = width // chunk
    others = freq_count // 2 - 1
    share = TU // freq_count
    pairs = row_count // 2
    total_blocks = row_count * blocks

    tile = block_owner[0, :, 0] * tiles_slab + tile_slot[0]
    ids = jnp.stack([tile // TILE_COLS, tile % TILE_COLS]).astype(jnp.float32)
    odd = lax.axis_index("row") % 2
    ids = jnp.concatenate([jnp.where(odd == 0, ids, 0.0), jnp.where(odd == 1, ids, 0.0)], axis=1)
    ids = jnp.pad(ids, ((0, 14), (0, 2 * TV - 2 * blocks)))
    x = jnp.broadcast_to((channel_freq - 1.284) / 0.428, (16, 2 * TV))
    scale = 1.0 / math.sqrt(blocks * row_count * vis_count)
    dma = pltpu.SemaphoreType.DMA
    with jax.named_scope("image"):
        image = pl.pallas_call(
            partial(image_kernel, freq_count, row_count),
            out_shape=jax.ShapeDtypeStruct((3, share, BANDS, width), jnp.bfloat16),
            in_specs=[vmem] * 9 + [pl.BlockSpec(memory_space=pl.ANY)] * 2,
            out_specs=vmem,
            scratch_shapes=[
                pltpu.VMEM((2 * TU, blocks, TV), jnp.float32),
                pltpu.VMEM((2, row_count, TU * blocks + 16, 2 * TV), jnp.bfloat16),
                pltpu.VMEM((chunks, 2 * TV, 2 * chunk), jnp.bfloat16),
                pltpu.VMEM((BANDS // 16, TU // 2 * 16, 2 * TU * 16), jnp.bfloat16),
                pltpu.VMEM((2 * BANDS, 2 * total_blocks), jnp.bfloat16),
                pltpu.VMEM((total_blocks, 2 * chunk), jnp.float32),
                pltpu.VMEM((2 * TU, BANDS, chunk), jnp.bfloat16),
                pltpu.VMEM((2, chunks, TU // 2, BANDS, chunk), jnp.bfloat16),
                pltpu.VMEM((2, chunks, others, share, BANDS, chunk), jnp.bfloat16),
                pltpu.VMEM((16, chunk), jnp.float32),
                pltpu.VMEM((others, 16, chunk), jnp.float32),
                dma((2,)),
                dma((2,)),
                dma((2, pairs - 1)),
                dma((2, pairs - 1)),
                dma((2, pairs)),
                dma((2, pairs)),
                dma((2, chunks, others)),
                dma((2, chunks, others)),
                dma((others,)),
                dma((others,)),
            ],
            compiler_params=pltpu.CompilerParams(
                vmem_limit_bytes=VMEM_LIMIT, collective_id=0, has_side_effects=True
            ),
        )(
            vis_values,
            kernel_u,
            kernel_v,
            offset_u,
            offset_v,
            ids,
            x,
            phase_table(chunk),
            band_table(scale),
            tile_tables(row_count, chunk),
            inner_table(),
        )
    return image.reshape(3, GRID // freq_count, width)


def solution(mesh):
    return jax.shard_map(
        shards,
        mesh=mesh,
        in_specs=(
            P("freq", "row", None, None),
            P("freq", "row", None, None),
            P("freq", "row", None, None),
            P("freq", "row", None),
            P("freq", "row", None),
            P("freq", "row", None),
            P("freq", "row"),
            P("freq"),
        ),
        out_specs=P(None, "freq", "row"),
        check_vma=False,
    )
```

time: 189 us -> 139 us (0.74)
  waiting for transfers between devices: 36.5 us -> 0 us
  between operations: 14.1 us -> 0.67 us
  Pallas kernels: 125 us -> 127 us
    all_gather x1 -> x0, waiting for transfers between devices: 36.5 us -> none  [shards(): tiles = lax.all_gather(tiles, 'row')]
    squeeze x4 -> x0, local copies, waits for them, and re-layouts: 5.01 us -> none  [the longest x1 1.89 us: shards(): lax.dynamic_index_in_dim(jnp.asarray(tile_tables(row_count, chunk)), lax....]
    unnamed x1 -> x3, local copies, waits for them, and re-layouts: 3.76 us -> 7.01 us
    pallas_call x2 -> x1, Pallas kernels: 125 us -> 127 us  [shards(): pl.pallas_call(partial(image_kernel, freq_count, row_count), out_shape=ja...]
  transfers between devices with their start and end apart: 1 -> 0, of which waited for: 1 -> 0; matrix products, arithmetic and copies ran while one was open for 1% -> 0% of each run, Pallas kernels for 0% -> 0%
where the time goes in v3:
time: 139 us; the launch traced here: 137 us
  Pallas kernels  127 us (91%)
  local copies, waits for them, and re-layouts  7.61 us (5%)
    pallas_call x1, Pallas kernels, shards(): pl.pallas_call(partial(image_kernel, freq_count, row_count), out_shape=ja...  127 us
    unnamed x3, local copies, waits for them, and re-layouts  7.01 us

profile of v3, /device:TPU:16, one launch (start us, length us, event | category | flops | bytes accessed | tf_op | source)
XLA Modules:
  0.0 137.1 jit_solution(7195286904054841227)
XLA Ops:
  0.7 0.7 and_select_fusion.1
  1.4 0.7 select_maximum_fusion.ids_ref
  2.0 0.6 broadcast_in_dim.11.x_ref
  2.6 1.6 %copy.13.ku_ref = bf16[1,64,7,128]{3,2,1,0:T(8,128)(2,1)} copy(bf16[1,64,7,128]{3,1,2,0:T(8,128)(2,1)} %param.13) | data formatting | bytes 229376 | tf_op args[1]
  4.3 1.6 %copy.14.kv_ref = bf16[1,64,7,128]{3,2,1,0:T(8,128)(2,1)} copy(bf16[1,64,7,128]{3,1,2,0:T(8,128)(2,1)} %param.14) | data formatting | bytes 229376 | tf_op args[2]
  5.9 127.5 %image.1 = bf16[3,4,256,512]{3,2,1,0:T(8,128)(2,1)} custom-call(bf16[1,64,2,128]{3,2,1,0:T(2,128)(2,1)} %vis_ref.1, bf16[1,64,7,128]{3,2,1,0:T(8,128)(2,1)} %copy.13.ku_ref, bf16[1,64,7,128]{3,2,1,0:T(8,128)(2,1)} %copy.14.kv_ref, s32[1,64,128]{2,1,0:T(8,128)} %ou_ref.1, s32[1,64,128]{2,1,0:T(8,128)} %ov_ref.1, f32[16,256]{1,0:T(8,128)} %select_maximum_fusion.ids_ref, ...), custom_call_target="tpu_custom_call" | custom-call | tf_op jit(solution)/shard_map/image/pallas_call | solution.py:375
  133.4 3.8 %copy.17 = bf16[3,1024,512]{2,1,0:T(8,128)(2,1)} copy(bf16[3,1024,512]{2,1,0:T(8,128)(2,1)} %bitcast.9) | data formatting | bytes 6291456
  (2 shorter events, 0.0 us)

commit v4 on v3

--- a/solution.py
+++ b/solution.py
@@ -37,9 +37,7 @@
 
 def phase_table(chunk):
     cos, sin = turn(np.arange(TILE_COLS)[:, None] * np.arange(chunk)[None, :], TILE_COLS)
-    whole = np.concatenate([cos, sin], axis=1).astype(np.float32)
-    main = whole.astype(BF16)
-    return np.concatenate([main, (whole - main.astype(np.float32)).astype(BF16)], axis=0)
+    return np.concatenate([cos, sin], axis=1).astype(BF16)
 
 
 def band_table(scale):
@@ -60,20 +58,20 @@
     return full.reshape(groups, TU * 16, TU * 2 * 16).astype(BF16)
 
 
-def grid_tiles(vis_ref, ku_ref, kv_ref, ou_ref, ov_ref, tile_ref):
-    blocks, taps = ku_ref.shape[1], ku_ref.shape[2]
+def grid_tiles(vis_ref, ku_ref, kv_ref, ou_ref, ov_ref, ku_wide, kv_wide, tile_ref):
+    taps, blocks = ku_ref.shape[:2]
+    ku_wide[...] = ku_ref[...].astype(jnp.float32)
+    kv_wide[...] = kv_ref[...].astype(jnp.float32)
 
     def one(b, carry):
         d_u = lax.broadcasted_iota(jnp.int32, (TU, TV), 0) - ou_ref[0, pl.ds(b, 1), :]
         d_v = lax.broadcasted_iota(jnp.int32, (TV, TV), 0) - ov_ref[0, pl.ds(b, 1), :]
-        ku = ku_ref[0, b].astype(jnp.float32)
-        kv = kv_ref[0, b].astype(jnp.float32)
         vis = vis_ref[0, b].astype(jnp.float32)
         spread_u = jnp.zeros((TU, TV), jnp.float32)
         spread_v = jnp.zeros((TV, TV), jnp.float32)
         for t in range(taps):
-            spread_u = jnp.where(d_u == t, ku[t : t + 1], spread_u)
-            spread_v = jnp.where(d_v == t, kv[t : t + 1], spread_v)
+            spread_u = jnp.where(d_u == t, ku_wide[t, pl.ds(b, 1), :], spread_u)
+            spread_v = jnp.where(d_v == t, kv_wide[t, pl.ds(b, 1), :], spread_v)
         left = jnp.concatenate([vis[0:1] * spread_u, vis[1:2] * spread_u], axis=0)
         tile = lax.dot_general(
             left.astype(jnp.bfloat16),
@@ -104,6 +102,8 @@
     tile_table_hbm,
     inner_hbm,
     out_ref,
+    ku_wide,
+    kv_wide,
     grid_ref,
     tiles_ref,
     tile_table_ref,
@@ -155,7 +155,7 @@
     for copy in tables:
         copy.start()
 
-    grid_tiles(vis_ref, ku_ref, kv_ref, ou_ref, ov_ref, grid_ref)
+    grid_tiles(vis_ref, ku_ref, kv_ref, ou_ref, ov_ref, ku_wide, kv_wide, grid_ref)
     for i in range(TU):
         rows = slice(i * block_count, (i + 1) * block_count)
         tiles_ref[0, row, rows, :TV] = grid_ref[i].astype(jnp.bfloat16)
@@ -257,14 +257,13 @@
             factor_ref[:BANDS, imag_lanes] = -picked[BANDS:]
             factor_ref[BANDS:, lanes] = picked[BANDS:]
             factor_ref[BANDS:, imag_lanes] = picked[:BANDS]
-            at = lax.broadcasted_iota(jnp.int32, (2 * TILE_COLS, TV), 0)
-            cols = (at == ids[1:2]) | (at == ids[1:2] + TILE_COLS)
+            cols = lax.broadcasted_iota(jnp.int32, (TILE_COLS, TV), 0) == ids[1:2]
             phase_ref[lanes, :] = lax.dot_general(
                 cols.astype(jnp.float32).astype(jnp.bfloat16),
                 phase_table_ref[...],
                 (((0,), (0,)), ((), ())),
                 preferred_element_type=jnp.float32,
-            )
+            ).astype(jnp.bfloat16)
 
         copies = []
         for q in range(chunks):
@@ -273,20 +272,17 @@
                 rows = pl.ds(pl.multiple_of(i * block_count, block_count), block_count)
                 tiles = tiles_ref[c, :, rows, :].reshape(blocks, 2 * TV)
                 cols = jnp.dot(tiles, tile_table_ref[q], preferred_element_type=jnp.float32)
+                cols = cols.astype(jnp.bfloat16)
                 real, imag = cols[:, :chunk], cols[:, chunk:]
                 cos, sin = phase_ref[:, :chunk], phase_ref[:, chunk:]
                 turned = jnp.concatenate(
-                    [
-                        (real * cos - imag * sin).astype(jnp.bfloat16),
-                        (real * sin + imag * cos).astype(jnp.bfloat16),
-                    ],
-                    axis=0,
+                    [real * cos - imag * sin, real * sin + imag * cos], axis=0
                 )
                 y = jnp.dot(factor_ref[...], turned, preferred_element_type=jnp.float32)
                 mid_ref[pl.ds(2 * i, 2)] = y.astype(jnp.bfloat16).reshape(2, BANDS, chunk)
                 return carry
 
-            lax.fori_loop(0, TU, first, 0)
+            lax.fori_loop(0, TU, first, 0, unroll=4)
 
             def second(g, carry):
                 rows = pl.ds(pl.multiple_of(g * 16, 16), 16)
@@ -295,7 +291,7 @@
                 send_ref[c, q, :, rows, :] = z.astype(jnp.bfloat16).reshape(TU // 2, 16, chunk)
                 return carry
 
-            lax.fori_loop(0, BANDS // 16, second, 0)
+            lax.fori_loop(0, BANDS // 16, second, 0, unroll=4)
             for n, peer in enumerate(group):
                 copies.append(
                     remote(
@@ -353,6 +349,7 @@
     freq_count = lax.axis_size("freq")
     blocks = vis_values.shape[1]
     vis_count = vis_values.shape[3]
+    taps = kernel_u.shape[2]
     width = GRID // row_count
     tiles_slab = GRID // row_count // TU * TILE_COLS
     vmem = pl.BlockSpec(memory_space=pltpu.VMEM)
@@ -378,12 +375,14 @@
             in_specs=[vmem] * 9 + [pl.BlockSpec(memory_space=pl.ANY)] * 2,
             out_specs=vmem,
             scratch_shapes=[
+                pltpu.VMEM((taps, blocks, TV), jnp.float32),
+                pltpu.VMEM((taps, blocks, TV), jnp.float32),
                 pltpu.VMEM((2 * TU, blocks, TV), jnp.float32),
                 pltpu.VMEM((2, row_count, TU * blocks + 16, 2 * TV), jnp.bfloat16),
                 pltpu.VMEM((chunks, 2 * TV, 2 * chunk), jnp.bfloat16),
                 pltpu.VMEM((BANDS // 16, TU // 2 * 16, 2 * TU * 16), jnp.bfloat16),
                 pltpu.VMEM((2 * BANDS, 2 * total_blocks), jnp.bfloat16),
-                pltpu.VMEM((total_blocks, 2 * chunk), jnp.float32),
+                pltpu.VMEM((total_blocks, 2 * chunk), jnp.bfloat16),
                 pltpu.VMEM((2 * TU, BANDS, chunk), jnp.bfloat16),
                 pltpu.VMEM((2, chunks, TU // 2, BANDS, chunk), jnp.bfloat16),
                 pltpu.VMEM((2, chunks, others, share, BANDS, chunk), jnp.bfloat16),
@@ -405,8 +404,8 @@
             ),
         )(
             vis_values,
-            kernel_u,
-            kernel_v,
+            kernel_u[0].transpose(1, 0, 2),
+            kernel_v[0].transpose(1, 0, 2),
             offset_u,
             offset_v,
             ids,

time: 139 us -> 104 us (0.75)
  Pallas kernels: 127 us -> 95.5 us
  local copies, waits for them, and re-layouts: 7.61 us -> 4.36 us
    pallas_call x1, Pallas kernels: 127 us -> 95.5 us  [shards(): pl.pallas_call(partial(image_kernel, freq_count, row_count), out_shape=ja...]
    unnamed x3 -> x1, local copies, waits for them, and re-layouts: 7.01 us -> 3.76 us
where the time goes in v4:
time: 104 us; the launch traced here: 102 us
  Pallas kernels  95.5 us (92%)
  local copies, waits for them, and re-layouts  4.36 us (4%)
  other arithmetic  1.38 us (1%)
    pallas_call x1, Pallas kernels, shards(): pl.pallas_call(partial(image_kernel, freq_count, row_count), out_shape=ja...  95.5 us
    unnamed x1, local copies, waits for them, and re-layouts  3.76 us

profile of v4, /device:TPU:16, one launch (start us, length us, event | category | flops | bytes accessed | tf_op | source)
XLA Modules:
  0.0 101.9 jit_solution(8899983348438429836)
XLA Ops:
  0.7 0.7 and_select_fusion.1
  1.4 0.7 select_maximum_fusion.ids_ref
  2.0 0.6 broadcast_in_dim.11.x_ref
  2.6 95.5 %image.1 = bf16[3,4,256,512]{3,2,1,0:T(8,128)(2,1)} custom-call(bf16[1,64,2,128]{3,2,1,0:T(2,128)(2,1)} %vis_ref.1, bf16[7,64,128]{2,1,0:T(8,128)(2,1)} %bitcast.16, bf16[7,64,128]{2,1,0:T(8,128)(2,1)} %bitcast.17, s32[1,64,128]{2,1,0:T(8,128)} %ou_ref.1, s32[1,64,128]{2,1,0:T(8,128)} %ov_ref.1, f32[16,256]{1,0:T(8,128)} %select_maximum_fusion.ids_ref, ...), custom_call_target="tpu_custom_call" | custom-call | tf_op jit(solution)/shard_map/image/pallas_call | solution.py:372
  98.2 3.8 %copy.15 = bf16[3,1024,512]{2,1,0:T(8,128)(2,1)} copy(bf16[3,1024,512]{2,1,0:T(8,128)(2,1)} %bitcast.15) | data formatting | bytes 6291456
  (2 shorter events, 0.0 us)

commit v5 on v4

--- a/solution.py
+++ b/solution.py
@@ -58,10 +58,8 @@
     return full.reshape(groups, TU * 16, TU * 2 * 16).astype(BF16)
 
 
-def grid_tiles(vis_ref, ku_ref, kv_ref, ou_ref, ov_ref, ku_wide, kv_wide, tile_ref):
-    taps, blocks = ku_ref.shape[:2]
-    ku_wide[...] = ku_ref[...].astype(jnp.float32)
-    kv_wide[...] = kv_ref[...].astype(jnp.float32)
+def grid_tiles(first, count, vis_ref, ou_ref, ov_ref, ku_wide, kv_wide, tile_ref):
+    taps = ku_wide.shape[0]
 
     def one(b, carry):
         d_u = lax.broadcasted_iota(jnp.int32, (TU, TV), 0) - ou_ref[0, pl.ds(b, 1), :]
@@ -84,7 +82,7 @@
             tile_ref[TU + i, pl.ds(b, 1), :] = tile[TU + i : TU + i + 1]
         return carry
 
-    lax.fori_loop(0, blocks, one, 0, unroll=4)
+    lax.fori_loop(first, first + count, one, 0, unroll=4)
 
 
 def image_kernel(
@@ -138,8 +136,18 @@
     pairs = row_count // 2
     pair, sub = row // 2, lax.rem(row, 2)
     sibling = pair * 2 + 1 - sub
-    targets = [lax.rem(pair + d, pairs) * 2 + sub for d in range(1, pairs)]
-    sources = [lax.rem(pair + pairs - d, pairs) * 2 + sub for d in range(1, pairs)]
+    tree = pairs == 4
+    if tree:
+        y, x = pair // 2, lax.rem(pair, 2)
+        sources = [
+            (y * 2 + 1 - x) * 2 + sub,
+            ((1 - y) * 2 + x) * 2 + sub,
+            ((1 - y) * 2 + 1 - x) * 2 + sub,
+        ]
+        targets = sources[:2]
+    else:
+        sources = [lax.rem(pair + pairs - d, pairs) * 2 + sub for d in range(1, pairs)]
+        targets = [lax.rem(pair + d, pairs) * 2 + sub for d in range(1, pairs)]
     everyone = [{"freq": f} for f in [partner] + group] + [{"row": r} for r in [sibling] + targets]
 
     barrier = pltpu.get_barrier_semaphore()
@@ -155,12 +163,21 @@
     for copy in tables:
         copy.start()
 
-    grid_tiles(vis_ref, ku_ref, kv_ref, ou_ref, ov_ref, ku_wide, kv_wide, grid_ref)
-    for i in range(TU):
-        rows = slice(i * block_count, (i + 1) * block_count)
-        tiles_ref[0, row, rows, :TV] = grid_ref[i].astype(jnp.bfloat16)
-        tiles_ref[0, row, rows, TV:] = grid_ref[TU + i].astype(jnp.bfloat16)
-    meta_rows = slice(TU * block_count, TU * block_count + 16)
+    part_blocks = block_count // 2
+
+    def grid_part(p):
+        first = p * part_blocks
+        grid_tiles(first, part_blocks, vis_ref, ou_ref, ov_ref, ku_wide, kv_wide, grid_ref)
+        for i in range(TU):
+            rows = slice(i * part_blocks, (i + 1) * part_blocks)
+            taken = slice(first, first + part_blocks)
+            tiles_ref[0, row, p, rows, :TV] = grid_ref[i, taken].astype(jnp.bfloat16)
+            tiles_ref[0, row, p, rows, TV:] = grid_ref[TU + i, taken].astype(jnp.bfloat16)
+
+    ku_wide[...] = ku_ref[...].astype(jnp.float32)
+    kv_wide[...] = kv_ref[...].astype(jnp.float32)
+    grid_part(0)
+    meta_rows = slice(TU * part_blocks, TU * part_blocks + 16)
     x = x_ref[...]
     x_main = x.astype(jnp.bfloat16).astype(jnp.float32)
     x_next = (x - x_main).astype(jnp.bfloat16).astype(jnp.float32)
@@ -168,7 +185,8 @@
     line = lax.broadcasted_iota(jnp.int32, (16, 2 * TV), 0)
     meta = jnp.where(line == 2, x_main, ids_ref[...])
     meta = jnp.where(line == 3, x_next, jnp.where(line == 4, x_last, meta))
-    tiles_ref[0, row, meta_rows, :] = meta.astype(jnp.bfloat16)
+    for p in range(2):
+        tiles_ref[0, row, p, meta_rows, :] = meta.astype(jnp.bfloat16)
 
     def remote(src, dst, send, recv, device):
         copy = pltpu.make_async_remote_copy(
@@ -182,47 +200,70 @@
         copy.start()
         return copy
 
-    def to_rows(c):
-        own = tiles_ref.at[c, row]
-        direct = [
-            remote(own, own, row_send.at[c, n], row_recv.at[c, n], {"row": target})
-            for n, target in enumerate(targets)
-        ]
-        return direct, [
-            remote(own, own, core_send.at[c, 0], core_recv.at[c, 0], {"row": sibling})
-        ]
-
-    def forward(c, direct):
-        passed = []
-        for n, source in enumerate(sources):
-            direct[n].wait_recv()
-            block = tiles_ref.at[c, source]
-            passed.append(
-                remote(
-                    block,
-                    block,
-                    core_send.at[c, n + 1],
-                    core_recv.at[c, n + 1],
-                    {"row": sibling},
+    direct, near = {}, {}
+
+    def to_rows(c, p):
+        own = tiles_ref.at[c, row, p]
+        for n, target in enumerate(targets):
+            direct[c, n, p] = remote(
+                own, own, row_send.at[c, n, p], row_recv.at[c, n, p], {"row": target}
+            )
+        near[c, 0, p] = remote(
+            own, own, core_send.at[c, 0, p], core_recv.at[c, 0, p], {"row": sibling}
+        )
+
+    def to_sibling(c, n, p):
+        direct[c, n, p].wait_recv()
+        block = tiles_ref.at[c, sources[n], p]
+        near[c, n + 1, p] = remote(
+            block, block, core_send.at[c, n + 1, p], core_recv.at[c, n + 1, p], {"row": sibling}
+        )
+
+    def relay(c, p):
+        for n in range(len(targets)):
+            to_sibling(c, n, p)
+            if tree and n == p:
+                block = tiles_ref.at[c, sources[n], p]
+                direct[c, 2, p] = remote(
+                    block, block, row_send.at[c, 2, p], row_recv.at[c, 2, p],
+                    {"row": targets[1 - n]},
                 )
-            )
-        return passed
+
+    def relay_last(c):
+        if tree:
+            for p in range(2):
+                to_sibling(c, 2, p)
+
+    def swap_part(p):
+        return remote(
+            tiles_ref.at[0, row, p],
+            tiles_ref.at[1, row, p],
+            swap_sem.at[0, p],
+            swap_sem.at[1, p],
+            {"freq": partner},
+        )
+
+    def all_near(c):
+        for n in range(pairs):
+            for p in range(2):
+                near[c, n, p].wait_recv()
 
     pl.semaphore_wait(barrier, len(everyone))
-    swap = remote(
-        tiles_ref.at[0, row],
-        tiles_ref.at[1, row],
-        swap_sem.at[0],
-        swap_sem.at[1],
-        {"freq": partner},
-    )
-    direct_a, near_a = to_rows(0)
-    near_a += forward(0, direct_a)
-    swap.wait_recv()
-    direct_b, near_b = to_rows(1)
+    swaps = [swap_part(0)]
+    to_rows(0, 0)
+    grid_part(1)
+    swaps.append(swap_part(1))
+    to_rows(0, 1)
+    relay(0, 0)
+    relay(0, 1)
+    swaps[0].wait_recv()
+    to_rows(1, 0)
+    relay_last(0)
+    swaps[1].wait_recv()
+    to_rows(1, 1)
 
     def x_of(c):
-        meta = tiles_ref[c, row, meta_rows, :].astype(jnp.float32)
+        meta = tiles_ref[c, row, 0, meta_rows, :].astype(jnp.float32)
         return meta[2:3] + (meta[3:4] + meta[4:5])
 
     x_own = [x_of(0)[:, :chunk], x_of(1)[:, :chunk]]
@@ -232,17 +273,16 @@
         remote(x_send_ref, x_recv_ref.at[n], x_send_sem.at[n], x_recv_sem.at[n], {"freq": peer})
         for n, peer in enumerate(group)
     ]
-    for copy in near_a:
-        copy.wait_recv()
+    all_near(0)
     for copy in tables:
         copy.wait()
 
-    def channel(c):
+    def channel(c, hooks):
         for p in range(pairs):
             at = meta_rows.start
             ids = (
-                tiles_ref[c, 2 * p, at : at + 16, :TV].astype(jnp.float32)
-                + tiles_ref[c, 2 * p + 1, at : at + 16, :TV].astype(jnp.float32)
+                tiles_ref[c, 2 * p, 0, at : at + 16, :TV].astype(jnp.float32)
+                + tiles_ref[c, 2 * p + 1, 0, at : at + 16, :TV].astype(jnp.float32)
             )
             ids = ids.astype(jnp.int32)
             lanes = slice(p * TV, (p + 1) * TV)
@@ -269,8 +309,8 @@
         for q in range(chunks):
 
             def first(i, carry):
-                rows = pl.ds(pl.multiple_of(i * block_count, block_count), block_count)
-                tiles = tiles_ref[c, :, rows, :].reshape(blocks, 2 * TV)
+                rows = pl.ds(pl.multiple_of(i * part_blocks, part_blocks), part_blocks)
+                tiles = tiles_ref[c, :, :, rows, :].reshape(blocks, 2 * TV)
                 cols = jnp.dot(tiles, tile_table_ref[q], preferred_element_type=jnp.float32)
                 cols = cols.astype(jnp.bfloat16)
                 real, imag = cols[:, :chunk], cols[:, chunk:]
@@ -283,6 +323,8 @@
                 return carry
 
             lax.fori_loop(0, TU, first, 0, unroll=4)
+            if q == 0:
+                hooks[0]()
 
             def second(g, carry):
                 rows = pl.ds(pl.multiple_of(g * 16, 16), 16)
@@ -302,17 +344,18 @@
                         {"freq": peer},
                     )
                 )
+            if q == 0:
+                hooks[1]()
         return copies
 
-    images = channel(0)
-    near_b += forward(1, direct_b)
-    for copy in near_b:
-        copy.wait_recv()
-    images += channel(1)
+    images = channel(0, (lambda: relay(1, 0), lambda: relay(1, 1)))
+    relay_last(1)
+    all_near(1)
+    images += channel(1, (lambda: None, lambda: None))
 
     for copy in x_copies:
         copy.wait()
-    for copy in direct_a + direct_b + near_a + near_b + [swap]:
+    for copy in swaps + list(direct.values()) + list(near.values()):
         copy.wait_send()
     step = 32
     for q in range(chunks):
@@ -378,7 +421,7 @@
                 pltpu.VMEM((taps, blocks, TV), jnp.float32),
                 pltpu.VMEM((taps, blocks, TV), jnp.float32),
                 pltpu.VMEM((2 * TU, blocks, TV), jnp.float32),
-                pltpu.VMEM((2, row_count, TU * blocks + 16, 2 * TV), jnp.bfloat16),
+                pltpu.VMEM((2, row_count, 2, TU * blocks // 2 + 16, 2 * TV), jnp.bfloat16),
                 pltpu.VMEM((chunks, 2 * TV, 2 * chunk), jnp.bfloat16),
                 pltpu.VMEM((BANDS // 16, TU // 2 * 16, 2 * TU * 16), jnp.bfloat16),
                 pltpu.VMEM((2 * BANDS, 2 * total_blocks), jnp.bfloat16),
@@ -389,11 +432,11 @@
                 pltpu.VMEM((16, chunk), jnp.float32),
                 pltpu.VMEM((others, 16, chunk), jnp.float32),
                 dma((2,)),
-                dma((2,)),
-                dma((2, pairs - 1)),
-                dma((2, pairs - 1)),
-                dma((2, pairs)),
-                dma((2, pairs)),
+                dma((2, 2)),
+                dma((2, pairs - 1, 2)),
+                dma((2, pairs - 1, 2)),
+                dma((2, pairs, 2)),
+                dma((2, pairs, 2)),
                 dma((2, chunks, others)),
                 dma((2, chunks, others)),
                 dma((others,)),

time: 104 us -> 95.9 us (0.922)
  Pallas kernels: 95.5 us -> 88.1 us
    pallas_call x1, Pallas kernels: 95.5 us -> 88.1 us  [shards(): pl.pallas_call(partial(image_kernel, freq_count, row_count), out_shape=ja...]
where the time goes in v5:
time: 95.9 us; the launch traced here: 94.5 us
  Pallas kernels  88.1 us (92%)
  local copies, waits for them, and re-layouts  4.36 us (5%)
  other arithmetic  1.38 us (1%)
    pallas_call x1, Pallas kernels, shards(): pl.pallas_call(partial(image_kernel, freq_count, row_count), out_shape=ja...  88.1 us
    unnamed x1, local copies, waits for them, and re-layouts  3.76 us

profile of v5, /device:TPU:16, one launch (start us, length us, event | category | flops | bytes accessed | tf_op | source)
XLA Modules:
  0.0 94.5 jit_solution(18407705833984487466)
XLA Ops:
  0.7 0.7 and_select_fusion.1
  1.4 0.7 select_maximum_fusion.ids_ref
  2.0 0.6 broadcast_in_dim.11.x_ref
  2.6 88.1 %image.1 = bf16[3,4,256,512]{3,2,1,0:T(8,128)(2,1)} custom-call(bf16[1,64,2,128]{3,2,1,0:T(2,128)(2,1)} %vis_ref.1, bf16[7,64,128]{2,1,0:T(8,128)(2,1)} %bitcast.16, bf16[7,64,128]{2,1,0:T(8,128)(2,1)} %bitcast.17, s32[1,64,128]{2,1,0:T(8,128)} %ou_ref.1, s32[1,64,128]{2,1,0:T(8,128)} %ov_ref.1, f32[16,256]{1,0:T(8,128)} %select_maximum_fusion.ids_ref, ...), custom_call_target="tpu_custom_call" | custom-call | tf_op jit(solution)/shard_map/image/pallas_call | solution.py:415
  90.8 3.8 %copy.15 = bf16[3,1024,512]{2,1,0:T(8,128)(2,1)} copy(bf16[3,1024,512]{2,1,0:T(8,128)(2,1)} %bitcast.15) | data formatting | bytes 6291456
  (2 shorter events, 0.0 us)

commit v6 on v5

--- a/solution.py
+++ b/solution.py
@@ -322,7 +322,7 @@
                 mid_ref[pl.ds(2 * i, 2)] = y.astype(jnp.bfloat16).reshape(2, BANDS, chunk)
                 return carry
 
-            lax.fori_loop(0, TU, first, 0, unroll=4)
+            lax.fori_loop(0, TU, first, 0, unroll=8)
             if q == 0:
                 hooks[0]()
 
@@ -333,7 +333,7 @@
                 send_ref[c, q, :, rows, :] = z.astype(jnp.bfloat16).reshape(TU // 2, 16, chunk)
                 return carry
 
-            lax.fori_loop(0, BANDS // 16, second, 0, unroll=4)
+            lax.fori_loop(0, BANDS // 16, second, 0, unroll=8)
             for n, peer in enumerate(group):
                 copies.append(
                     remote(

time: 95.9 us -> 95.2 us (level)
  no operation moved by 1% of the time
where the time goes in v6:
time: 95.2 us; the launch traced here: 93.8 us
  Pallas kernels  87.4 us (92%)
  local copies, waits for them, and re-layouts  4.36 us (5%)
  other arithmetic  1.38 us (1%)
    pallas_call x1, Pallas kernels, shards(): pl.pallas_call(partial(image_kernel, freq_count, row_count), out_shape=ja...  87.4 us
    unnamed x1, local copies, waits for them, and re-layouts  3.76 us

profile of v6, /device:TPU:16, one launch (start us, length us, event | category | flops | bytes accessed | tf_op | source)
XLA Modules:
  0.0 93.8 jit_solution(7663479386882010538)
XLA Ops:
  0.7 0.7 and_select_fusion.1
  1.4 0.7 select_maximum_fusion.ids_ref
  2.0 0.6 broadcast_in_dim.11.x_ref
  2.6 87.4 %image.1 = bf16[3,4,256,512]{3,2,1,0:T(8,128)(2,1)} custom-call(bf16[1,64,2,128]{3,2,1,0:T(2,128)(2,1)} %vis_ref.1, bf16[7,64,128]{2,1,0:T(8,128)(2,1)} %bitcast.16, bf16[7,64,128]{2,1,0:T(8,128)(2,1)} %bitcast.17, s32[1,64,128]{2,1,0:T(8,128)} %ou_ref.1, s32[1,64,128]{2,1,0:T(8,128)} %ov_ref.1, f32[16,256]{1,0:T(8,128)} %select_maximum_fusion.ids_ref, ...), custom_call_target="tpu_custom_call" | custom-call | tf_op jit(solution)/shard_map/image/pallas_call | solution.py:415
  90.1 3.8 %copy.15 = bf16[3,1024,512]{2,1,0:T(8,128)(2,1)} copy(bf16[3,1024,512]{2,1,0:T(8,128)(2,1)} %bitcast.15) | data formatting | bytes 6291456
  (2 shorter events, 0.0 us)
